TPU v7x, 32 devices: a whole 2x2x4 slice. The times are simulated.
32 devices in a mesh: rows: 8 (over z, x), seq: 4 (over y, core).
Axes of the slice: x: 2, y: 2, z: 4, core: 2. Of those that a mesh axis runs over, the one named last changes fastest.
Arguments:
- tokens: bfloat16 [96, 512, 768], P('rows', 'seq'), may hold values from -6 to 6
- seg_lengths: int32 [96, 6], P('rows'), may hold values from 1 to 256, 512 in all within a row
- w_query: bfloat16 [768, 768], replicated, may hold values from -0.25 to 0.25
- w_key: bfloat16 [768, 768], replicated, may hold values from -0.25 to 0.25
- w_value: bfloat16 [768, 768], replicated, may hold values from -0.21875 to 0.21875
- w_output: bfloat16 [768, 768], replicated, may hold values from -0.625 to 0.625
- w_inner: bfloat16 [768, 3072], replicated, may hold values from -0.21875 to 0.21875
- w_outer: bfloat16 [3072, 768], replicated, may hold values from -0.1875 to 0.1875
- gain_attn: bfloat16 [768], replicated, may hold values from 0.099609375 to 1.8984375
- gain_ffn: bfloat16 [768], replicated, may hold values from 0.099609375 to 1.8984375
- bucket_bias_table: bfloat16 [32, 12], replicated, may hold values from -4 to 4
- cotangent: bfloat16 [96, 512, 768], P('rows', 'seq'), may hold values from -6 to 6
Outputs:
- out_tokens: bfloat16 [96, 512, 768], P('rows', 'seq')
- grad_tokens: bfloat16 [96, 512, 768], P('rows', 'seq')
- grad_query: float32 [768, 768], replicated
- grad_key: float32 [768, 768], replicated
- grad_value: float32 [768, 768], replicated
- grad_output: float32 [768, 768], replicated
- grad_inner: float32 [768, 3072], replicated
- grad_outer: float32 [3072, 768], replicated
- grad_gain_attn: float32 [768], replicated
- grad_gain_ffn: float32 [768], replicated
- grad_table: float32 [32, 12], replicated
Inputs may be any that keep to these rules, and one draw needn't show every extreme that they name: `seg_lengths`: each row's 6 entries sum to 512; the last is the row's padding; the largest entry of each row is 256.
All inputs are finite; a program needn't handle non-finite values.
Results may differ from a plain program's by a relative error of at most 0.015.
The roundings to bfloat16 on the way count: a program that leaves them out, or rounds other values in their place, can miss the bound.
Values may be sent and summed in bfloat16 or wider, within the bound.
A program may use at most 384 MiB of HBM per device.

v0:
```python
import math

import jax
import jax.numpy as jnp
from jax import lax
from jax.sharding import PartitionSpec as P

MICRO = 3


EPSILON = 1e-06
THRESHOLDS = (12, 16, 23, 32, 46, 64, 91)
NEGATIVE = -1e30
GELU_SCALE = math.sqrt(2.0 / math.pi)
GELU_CUBIC = 0.044715


def bucket_of(offsets, bucket_count):
    distance = jnp.abs(offsets)
    levels = 8 + sum(((distance >= threshold).astype(jnp.int32) for threshold in THRESHOLDS))
    return jnp.where(offsets > 0, bucket_count // 2, 0) + jnp.where(distance < 8, distance, levels)


def segment_ids(seg_lengths, row_len):
    ends = jnp.cumsum(seg_lengths, axis=1)
    positions = jnp.arange(row_len, dtype=jnp.int32)
    return jnp.sum((positions[None, :, None] >= ends[:, None, :]).astype(jnp.int32), axis=2)


def gelu_value(values_in):
    return jax.nn.gelu(values_in, approximate=True)


def gelu_slope(values_in):
    tangent = jnp.tanh(GELU_SCALE * (values_in + GELU_CUBIC * values_in * values_in * values_in))
    return 0.5 * (1.0 + tangent) + 0.5 * values_in * (1.0 - tangent * tangent) * GELU_SCALE * (
        1.0 + 3.0 * GELU_CUBIC * values_in * values_in
    )


def apply_rms_scaling(values_in, gain_row):
    inverse = lax.rsqrt(jnp.mean(values_in * values_in, axis=-1, keepdims=True) + EPSILON)
    return (values_in * inverse * gain_row, inverse)


def norm_back(values_in, inverse, gain_row, grad_normed):
    weighted = grad_normed * gain_row
    inner_mean = jnp.mean(weighted * values_in, axis=-1, keepdims=True)
    grad_values = inverse * weighted - values_in * (inverse * inverse * inverse) * inner_mean
    grad_gain = jnp.sum(grad_normed * values_in * inverse, axis=(0, 1))
    return (grad_values, grad_gain)


def split_heads(array_in, head_count):
    return array_in.reshape(
        array_in.shape[0], array_in.shape[1], head_count, array_in.shape[2] // head_count
    )


def join_heads(array_in):
    return array_in.reshape(
        array_in.shape[0], array_in.shape[1], array_in.shape[2] * array_in.shape[3]
    )


def score_block(query_rows, key_rows, relative_position_bias, allowed, head_count):
    raw_scores = jnp.einsum(
        "rqhd,rkhd->rhqk",
        split_heads(query_rows, head_count),
        split_heads(key_rows, head_count),
        preferred_element_type=jnp.float32,
    )
    return jnp.where(allowed, raw_scores + relative_position_bias[None], NEGATIVE)


def project(rows_in, weight_in):
    return jnp.einsum("rtd,de->rte", rows_in, weight_in, preferred_element_type=jnp.float32)


def project_back(rows_in, weight_in):
    return jnp.einsum("rte,de->rtd", rows_in, weight_in, preferred_element_type=jnp.float32)


def outer_sum(left_rows, right_rows):
    return jnp.einsum("rtd,rte->de", left_rows, right_rows, preferred_element_type=jnp.float32)


def per_device(
    tokens,
    seg_lengths,
    w_query,
    w_key,
    w_value,
    w_output,
    w_inner,
    w_outer,
    gain_attn,
    gain_ffn,
    bucket_bias_table,
    cotangent,
):
    rows_dev, piece_len, model_width = tokens.shape
    seq_parts = lax.axis_size("seq")
    row_len = piece_len * seq_parts
    bucket_count, head_count = bucket_bias_table.shape
    batch_rows = rows_dev // MICRO
    gain_one = gain_attn.astype(jnp.float32)
    gain_two = gain_ffn.astype(jnp.float32)
    seg_all = segment_ids(seg_lengths, row_len)
    key_place = jnp.arange(row_len, dtype=jnp.int32)
    query_place = lax.axis_index("seq") * piece_len + jnp.arange(piece_len, dtype=jnp.int32)
    offsets = key_place[None, :] - query_place[:, None]
    bucket_indicator = (
        bucket_of(offsets, bucket_count)[None]
        == jnp.arange(bucket_count, dtype=jnp.int32)[:, None, None]
    ).astype(jnp.bfloat16)
    relative_position_bias = jnp.einsum(
        "zfu,zi->ifu", bucket_indicator, bucket_bias_table, preferred_element_type=jnp.float32
    )
    sum_query = jnp.zeros(w_query.shape, jnp.float32)
    sum_key = jnp.zeros(w_key.shape, jnp.float32)
    sum_value = jnp.zeros(w_value.shape, jnp.float32)
    sum_output = jnp.zeros(w_output.shape, jnp.float32)
    sum_inner = jnp.zeros(w_inner.shape, jnp.float32)
    sum_outer = jnp.zeros(w_outer.shape, jnp.float32)
    sum_gain_one = jnp.zeros((model_width,), jnp.float32)
    sum_gain_two = jnp.zeros((model_width,), jnp.float32)
    bucket_bias_sum = jnp.zeros((head_count, query_place.shape[0], row_len), jnp.float32)
    out_list = []
    grad_in_list = []
    for micro_step in range(MICRO):
        row_start = micro_step * batch_rows
        tokens_part = tokens[row_start : row_start + batch_rows]
        grad_part = cotangent[row_start : row_start + batch_rows]
        seg_rows = seg_all[row_start : row_start + batch_rows]
        tokens_here, grad_out = (tokens_part, grad_part)
        seg_query = lax.dynamic_slice_in_dim(
            seg_rows, lax.axis_index("seq") * piece_len, piece_len, 1
        )
        allowed = seg_query[:, None, :, None] == seg_rows[:, None, None, :]
        tokens_wide = tokens_here.astype(jnp.float32)
        normed_wide, inverse_one = apply_rms_scaling(tokens_wide, gain_one)
        normed = normed_wide.astype(jnp.bfloat16)
        query_rows = project(normed, w_query).astype(jnp.bfloat16)
        key_rows = project(normed, w_key).astype(jnp.bfloat16)
        value_rows = project(normed, w_value).astype(jnp.bfloat16)
        keys_all, values_all = (
            lax.all_gather(key_rows, "seq", axis=1, tiled=True),
            lax.all_gather(value_rows, "seq", axis=1, tiled=True),
        )
        attention_logits = score_block(
            query_rows, keys_all, relative_position_bias, allowed, head_count
        )
        top_score = jnp.max(attention_logits, axis=-1, keepdims=True)
        exps = jnp.exp(attention_logits - top_score)
        exp_total = jnp.sum(exps, axis=-1, keepdims=True)
        probs_low = (exps / exp_total).astype(jnp.bfloat16)
        log_total = top_score + jnp.log(exp_total)
        mixed = join_heads(
            jnp.einsum(
                "rhqk,rkhd->rqhd",
                probs_low,
                split_heads(values_all, head_count),
                preferred_element_type=jnp.float32,
            )
        ).astype(jnp.bfloat16)
        hidden = tokens_wide + project(mixed, w_output)
        normed_two_wide, inverse_two = apply_rms_scaling(hidden, gain_two)
        normed_two = normed_two_wide.astype(jnp.bfloat16)
        inner_pre = project(normed_two, w_inner)
        active = gelu_value(inner_pre).astype(jnp.bfloat16)
        result = (hidden + project(active, w_outer)).astype(jnp.bfloat16)
        sum_outer = sum_outer + outer_sum(active, grad_out)
        grad_active = project_back(grad_out, w_outer)
        grad_pre = (grad_active * gelu_slope(inner_pre)).astype(jnp.bfloat16)
        sum_inner = sum_inner + outer_sum(normed_two, grad_pre)
        grad_hidden_part, gain_part = norm_back(
            hidden, inverse_two, gain_two, project_back(grad_pre, w_inner)
        )
        sum_gain_two = sum_gain_two + gain_part
        grad_hidden = grad_out.astype(jnp.float32) + grad_hidden_part
        grad_branch = grad_hidden.astype(jnp.bfloat16)
        sum_output = sum_output + outer_sum(mixed, grad_branch)
        grad_mixed = project_back(grad_branch, w_output).astype(jnp.bfloat16)
        keys_back, values_back = (keys_all, values_all)
        attention_logits = score_block(
            query_rows, keys_back, relative_position_bias, allowed, head_count
        )
        weights = jnp.exp(attention_logits - log_total)
        probs_back = weights.astype(jnp.bfloat16)
        grad_mixed_heads = split_heads(grad_mixed, head_count)
        grad_values_all = join_heads(
            jnp.einsum(
                "rhqk,rqhd->rkhd", probs_back, grad_mixed_heads, preferred_element_type=jnp.float32
            )
        )
        grad_probs = jnp.einsum(
            "rqhd,rkhd->rhqk",
            grad_mixed_heads,
            split_heads(values_back, head_count),
            preferred_element_type=jnp.float32,
        )
        inner_total = jnp.sum(grad_probs * weights, axis=-1, keepdims=True)
        grad_scores = (weights * (grad_probs - inner_total)).astype(jnp.bfloat16)
        bucket_bias_sum = bucket_bias_sum + jnp.sum(grad_scores.astype(jnp.float32), axis=0)
        grad_query_rows = join_heads(
            jnp.einsum(
                "rhqk,rkhd->rqhd",
                grad_scores,
                split_heads(keys_back, head_count),
                preferred_element_type=jnp.float32,
            )
        ).astype(jnp.bfloat16)
        grad_keys_all = join_heads(
            jnp.einsum(
                "rhqk,rqhd->rkhd",
                grad_scores,
                split_heads(query_rows, head_count),
                preferred_element_type=jnp.float32,
            )
        )
        grad_key_rows, grad_value_rows = (
            lax.psum_scatter(
                grad_keys_all.astype(jnp.bfloat16), "seq", scatter_dimension=1, tiled=True
            ).astype(jnp.float32),
            lax.psum_scatter(
                grad_values_all.astype(jnp.bfloat16), "seq", scatter_dimension=1, tiled=True
            ).astype(jnp.float32),
        )
        grad_key_rows = grad_key_rows.astype(jnp.bfloat16)
        grad_value_rows = grad_value_rows.astype(jnp.bfloat16)
        sum_query = sum_query + outer_sum(normed, grad_query_rows)
        sum_key = sum_key + outer_sum(normed, grad_key_rows)
        sum_value = sum_value + outer_sum(normed, grad_value_rows)
        grad_normed = (
            project_back(grad_query_rows, w_query)
            + project_back(grad_key_rows, w_key)
            + project_back(grad_value_rows, w_value)
        )
        grad_tokens_part, gain_part = norm_back(tokens_wide, inverse_one, gain_one, grad_normed)
        sum_gain_one = sum_gain_one + gain_part
        grad_input = (grad_hidden + grad_tokens_part).astype(jnp.bfloat16)
        out_list.append(result)
        grad_in_list.append(grad_input)
    sum_table = jnp.einsum(
        "eml,aml->ea",
        bucket_indicator.astype(jnp.float32),
        bucket_bias_sum,
        precision=lax.Precision.HIGHEST,
    )
    grad_list = (
        sum_query,
        sum_key,
        sum_value,
        sum_output,
        sum_inner,
        sum_outer,
        sum_gain_one,
        sum_gain_two,
        sum_table,
    )
    flat_grads = jnp.concatenate([grad_piece.reshape(-1) for grad_piece in grad_list])
    devices = lax.axis_size("rows") * lax.axis_size("seq")
    pad_count = -flat_grads.shape[0] % (devices * 128)
    flat_grads = jnp.pad(flat_grads, (0, pad_count))
    share_len = flat_grads.shape[0] // devices
    flat_grads = flat_grads.reshape(share_len, devices).T.reshape(-1, 128)
    grad_scale = float(rows_dev * lax.axis_size("rows") * row_len) ** (-0.5)
    grad_share = (
        lax.psum_scatter(flat_grads, ("rows", "seq"), scatter_dimension=0, tiled=True) * grad_scale
    )
    summed_all = lax.all_gather(
        grad_share.astype(jnp.bfloat16), ("rows", "seq"), axis=0, tiled=True
    ).astype(grad_share.dtype)
    summed_all = summed_all.reshape(devices, share_len).T.reshape(-1)
    results = []
    offset_now = 0
    for grad_piece in grad_list:
        piece_count = grad_piece.size
        results.append(summed_all[offset_now : offset_now + piece_count].reshape(grad_piece.shape))
        offset_now += piece_count
    return (
        jnp.concatenate(out_list, axis=0),
        jnp.concatenate(grad_in_list, axis=0),
        results[0],
        results[1],
        results[2],
        results[3],
        results[4],
        results[5],
        results[6],
        results[7],
        results[8],
    )


def solution(mesh):
    in_specs = (
        P("rows", "seq", None),
        P("rows", None),
        P(),
        P(),
        P(),
        P(),
        P(),
        P(),
        P(),
        P(),
        P(),
        P("rows", "seq", None),
    )
    out_specs = (
        P("rows", "seq", None),
        P("rows", "seq", None),
        P(),
        P(),
        P(),
        P(),
        P(),
        P(),
        P(),
        P(),
        P(),
    )
    return jax.shard_map(
        per_device, mesh=mesh, in_specs=in_specs, out_specs=out_specs, check_vma=False
    )
```

profile of v0, /device:TPU:1, one launch (start us, length us, event | category | flops | bytes accessed | tf_op | source)
XLA Modules:
  0.0 1432.1 jit_solution(15668726695675343329)
XLA Ops:
  35.7 37.5 %copy.302 = pred[32,128,512]{2,0,1:T(32,128)(4,1)S(1)} copy(pred[32,128,512]{1,0,2:T(32,128)(4,1)S(1)} %iota_compare_fusion) | data formatting | bytes 4194304 | tf_op jit(solution)/shard_map/eq | solution.py:114
  114.7 8.5 fusion.131
  130.7 10.9 fusion.227
  146.9 21.0 %all-gather.11.cloned.1.call-done = bf16[4,512,768]{2,1,0:T(8,128)(2,1)} async-done(((bf16[4,128,768]{2,1,0:T(8,128)(2,1)}), bf16[4,512,768]{2,1,0:T(8,128)(2,1)}) %all-gather.11.cloned.1.call-update) | async-done | bytes 3145744 | tf_op jit(solution)/shard_map/all_gather | solution.py:148
  172.6 8.1 fusion.2
  207.3 7.7 fusion.133
  221.5 9.0 fusion.52
  249.9 7.1 fusion.38
  267.5 12.5 multiply_reduce_fusion.1
  280.6 8.7 convert_reduce_fusion.1
  304.2 15.4 %multiply_reduce_fusion.2 = (f32[4,12,128]{2,1,0:T(8,128)S(1)}, f32[4,12,128,512]{3,2,1,0:T(8,128)}) fusion(f32[4,12,128,512]{3,2,1,0:T(8,128)} %copy-done.3, f32[4,12,128]{2,1,0:T(8,128)S(1)} %log_add_fusion.2, bf16[4,128,12,64]{1,3,2,0:T(8,128)(2,1)} %bitcast.326, bf16[4,512,12,64]{1,3,2,0:T(8,128)(2,1)} %bitcast.311), kind=kOutput, calls=%fused_computation.11 | convolution fusion | flops 412084224 | bytes 29147136 | tf_op jit(solution)/shard_map/rqhd,rkhd->rhqk/dot_general | solution.py:197
  319.6 8.6 convert_reduce_fusion.2
  342.1 13.4 multiply_reduce_fusion
  357.7 8.6 convert_reduce_fusion
  375.4 7.1 fusion.89
  388.4 7.2 fusion.86
  400.2 7.1 fusion.92
  442.4 7.3 fusion.190
  456.4 9.4 fusion.7
  477.5 10.3 fusion.168
  487.8 9.0 bitcast_add_fusion
  496.8 10.8 reshape.404
  507.6 6.7 add_add_fusion
  559.8 12.7 reduce-scatter.19.cloned.1.call-done
  588.1 9.6 constant_dynamic-update-slice_fusion.4
  607.6 6.8 fusion.124
  616.6 10.0 pad.4
  626.6 66.7 %reshape.406 = f32[221312,32]{1,0:T(8,128)} reshape(f32[7081984]{0:T(1024)} %pad.4) | data formatting | bytes 56655872 | tf_op jit(solution)/shard_map/reshape | solution.py:267
  693.2 66.8 %copy.345 = f32[32,221312]{1,0:T(8,128)} copy(f32[32,221312]{0,1:T(8,128)} %bitcast.69) | data formatting | bytes 56655872 | tf_op jit(solution)/shard_map/transpose | solution.py:267
  760.1 27.3 %reshape.407 = f32[55328,128]{1,0:T(8,128)} reshape(f32[32,221312]{1,0:T(8,128)} %copy.345) | data formatting | bytes 56655872 | tf_op jit(solution)/shard_map/reshape | solution.py:267
  787.3 305.7 %fusion = f32[1744,128]{1,0:T(8,128)} fusion(f32[55328,128]{1,0:T(8,128)} %reshape.407), kind=kCustom, calls=%all-reduce-scatter | all-reduce-scatter fusion | flops 7143425 | bytes 29220864
  1109.9 8.5 add_convert_fusion
  1118.4 8.3 add_convert_fusion.1
  1137.2 80.1 %all-gather.21.cloned.1.call-done = bf16[32,1729,128]{2,1,0:T(8,128)(2,1)} async-done(((bf16[1,1729,128]{2,1,0:T(8,128)(2,1)}), bf16[32,1729,128]{2,1,0:T(8,128)(2,1)}) %all-gather.21.cloned.1.call-update) | async-done | bytes 14163984 | tf_op jit(solution)/shard_map/all_gather | solution.py:272
  1217.3 33.1 %copy.385 = f32[4,8,1729,128]{3,1,2,0:T(8,128)} copy(bf16[4,8,1729,128]{3,2,1,0:T(8,128)(2,1)} %bitcast.305) | data formatting | bytes 42491904
  1250.4 6.9 fusion.224
  1257.3 13.4 fusion.223
  1272.9 6.7 copy.346
  1279.6 7.4 reshape.409
  1287.0 6.7 copy.347
  1293.7 7.4 reshape.410
  1301.1 6.7 copy.348
  1307.8 7.4 reshape.411
  1320.3 7.4 reshape.412
  1327.7 20.9 %copy.350 = f32[73728,32]{1,0:T(8,128)} copy(f32[73728,32]{0,1:T(8,128)} %get-tuple-element.94) | data formatting | bytes 18874368 | tf_op jit(solution)/shard_map/slice | solution.py:280
  1348.6 27.7 %reshape.413 = f32[768,3072]{1,0:T(8,128)} reshape(f32[73728,32]{1,0:T(8,128)} %copy.350) | data formatting | bytes 18874368 | tf_op jit(solution)/shard_map/reshape | solution.py:280
  1376.3 20.9 %copy.351 = f32[73728,32]{1,0:T(8,128)} copy(f32[73728,32]{0,1:T(8,128)} %get-tuple-element.93) | data formatting | bytes 18874368 | tf_op jit(solution)/shard_map/slice | solution.py:280
  1397.2 25.9 %reshape.414 = f32[3072,768]{1,0:T(8,128)} reshape(f32[73728,32]{1,0:T(8,128)} %copy.351) | data formatting | bytes 18874368 | tf_op jit(solution)/shard_map/reshape | solution.py:280
  (468 shorter events, 364.0 us)
Async XLA Ops:
  7.2 83.8 %all-gather.19.cloned.1.call-start = ((), (), s32[]{:S(2)}) async-start(), calls=%async_computation.11 | async-start | bytes 3932160 | tf_op jit(solution)/shard_map/all_gather | solution.py:148
  10.9 21.6 %copy-start.79 = (f32[768]{0:T(1024)}, f32[768]{0:T(1024)S(1)}, u32[]{:S(2)}) copy-start(f32[768]{0:T(1024)S(1)} %convert_element_type.340) | copy-start | bytes 9220
  11.5 16.2 %copy-start.84 = (f32[4,128]{1,0:T(4,128)}, f32[4,128]{1,0:T(4,128)S(1)}, u32[]{:S(2)}) copy-start(f32[4,128]{1,0:T(4,128)S(1)} %get-tuple-element.117) | copy-start | bytes 6148
  11.5 19.3 %copy-start.90 = (f32[4,128]{1,0:T(4,128)}, f32[4,128]{1,0:T(4,128)S(1)}, u32[]{:S(2)}) copy-start(f32[4,128]{1,0:T(4,128)S(1)} %get-tuple-element.144) | copy-start | bytes 6148
  14.7 95.3 %all-gather.17.cloned.1.call-start = ((), (), s32[]{:S(2)}) async-start(), calls=%async_computation.10 | async-start | bytes 3932160 | tf_op jit(solution)/shard_map/all_gather | solution.py:149
  16.6 109.5 %all-gather.15.cloned.1.call-start = ((), (), s32[]{:S(2)}) async-start(), calls=%async_computation.9 | async-start | bytes 3932160 | tf_op jit(solution)/shard_map/all_gather | solution.py:148
  19.6 122.5 %all-gather.13.cloned.1.call-start = ((), (), s32[]{:S(2)}) async-start(), calls=%async_computation.8 | async-start | bytes 3932160 | tf_op jit(solution)/shard_map/all_gather | solution.py:149
  21.4 146.5 %all-gather.11.cloned.1.call-start = ((), (), s32[]{:S(2)}) async-start(), calls=%async_computation.7 | async-start | bytes 3932160 | tf_op jit(solution)/shard_map/all_gather | solution.py:148
  22.7 9.8 copy-start.87
  25.8 176.9 %all-gather.9.cloned.1.call-start = ((), (), s32[]{:S(2)}) async-start(), calls=%async_computation.6 | async-start | bytes 3932160 | tf_op jit(solution)/shard_map/all_gather | solution.py:149
  27.6 509.7 %reduce-scatter.13.cloned.1.call-start = ((), (), s32[]{:S(2)}) async-start(), calls=%async_computation.14 | async-start | bytes 3932160 | tf_op jit(solution)/shard_map/reduce_scatter | solution.py:223
  34.5 38.7 %copy-start.103 = (bf16[32,12]{0,1:T(8,128)(2,1)S(1)}, bf16[32,12]{0,1:T(8,128)(2,1)}, u32[]{:S(2)}) copy-start(bf16[32,12]{0,1:T(8,128)(2,1)} %param.22) | copy-start | bytes 2308
  216.0 44.8 %copy-start.20 = (f32[4,128,768]{2,1,0:T(8,128)}, f32[4,128,768]{2,1,0:T(8,128)S(1)}, u32[]{:S(2)}) copy-start(f32[4,128,768]{2,1,0:T(8,128)S(1)} %get-tuple-element.135) | copy-start | bytes 4718596
  216.8 13.8 slice-start.13
  216.8 19.2 %slice-start.22 = ((s8[4718592]{0:T(1024)(128)(4,1)}), s8[4194304]{0:T(1024)(128)(4,1)S(1)}, s32[]{:S(2)}) async-start(s8[4718592]{0:T(1024)(128)(4,1)} %bitcast.344), calls=%async_computation.41 | async-start | bytes 8388608
  221.5 14.5 %slice-start.23 = ((s8[4718592]{0:T(1024)(128)(4,1)}), s8[524288]{0:T(1024)(128)(4,1)S(1)}, s32[]{:S(2)}) async-start(s8[4718592]{0:T(1024)(128)(4,1)} %bitcast.344), calls=%async_computation.42 | async-start | bytes 1048576
  263.1 73.7 %copy-start.24 = (f32[4,128,768]{2,1,0:T(8,128)}, f32[4,128,768]{2,1,0:T(8,128)S(1)}, u32[]{:S(2)}) copy-start(f32[4,128,768]{2,1,0:T(8,128)S(1)} %get-tuple-element.104) | copy-start | bytes 4718596
  267.5 12.5 slice-start.3
  267.5 12.5 slice-start.4
  267.5 13.1 slice-start.5
  267.5 13.1 copy-start.70
  297.6 243.3 %reduce-scatter.9.cloned.1.call-start = ((), (), s32[]{:S(2)}) async-start(), calls=%async_computation.12 | async-start | bytes 3932160 | tf_op jit(solution)/shard_map/reduce_scatter | solution.py:223
  304.1 15.5 %copy-start.72 = (f32[4,12,128]{2,1,0:T(8,128)}, f32[4,12,128]{2,1,0:T(8,128)S(1)}, u32[]{:S(2)}) copy-start(f32[4,12,128]{2,1,0:T(8,128)S(1)} %log_add_fusion.2) | copy-start | bytes 73732
  304.1 15.4 %slice-start.6 = ((s8[12582912]{0:T(1024)(128)(4,1)}), s8[4194304]{0:T(1024)(128)(4,1)S(1)}, s32[]{:S(2)}) async-start(s8[12582912]{0:T(1024)(128)(4,1)} %bitcast.282), calls=%async_computation.25 | async-start | bytes 8388608
  304.1 15.4 %slice-start.7 = ((s8[12582912]{0:T(1024)(128)(4,1)}), s8[4194304]{0:T(1024)(128)(4,1)S(1)}, s32[]{:S(2)}) async-start(s8[12582912]{0:T(1024)(128)(4,1)} %bitcast.282), calls=%async_computation.26 | async-start | bytes 8388608
  304.2 15.4 %slice-start.8 = ((s8[12582912]{0:T(1024)(128)(4,1)}), s8[4194304]{0:T(1024)(128)(4,1)S(1)}, s32[]{:S(2)}) async-start(s8[12582912]{0:T(1024)(128)(4,1)} %bitcast.282), calls=%async_computation.27 | async-start | bytes 8388608
  336.5 207.7 %reduce-scatter.17.cloned.1.call-start = ((), (), s32[]{:S(2)}) async-start(), calls=%async_computation.16 | async-start | bytes 3932160 | tf_op jit(solution)/shard_map/reduce_scatter | solution.py:223
  342.0 13.4 copy-start.74
  342.0 13.4 slice-start
  342.1 13.4 slice-start.1
  342.1 15.6 %slice-start.2 = ((s8[12582912]{0:T(1024)(128)(4,1)}), s8[4194304]{0:T(1024)(128)(4,1)S(1)}, s32[]{:S(2)}) async-start(s8[12582912]{0:T(1024)(128)(4,1)} %bitcast.278), calls=%async_computation.21 | async-start | bytes 8388608
  374.6 178.2 %reduce-scatter.15.cloned.1.call-start = ((), (), s32[]{:S(2)}) async-start(), calls=%async_computation.15 | async-start | bytes 3932160 | tf_op jit(solution)/shard_map/reduce_scatter | solution.py:226
  387.1 169.2 %reduce-scatter.11.cloned.1.call-start = ((), (), s32[]{:S(2)}) async-start(), calls=%async_computation.13 | async-start | bytes 3932160 | tf_op jit(solution)/shard_map/reduce_scatter | solution.py:226
  407.3 12.9 slice-start.9
  455.0 117.4 %reduce-scatter.19.cloned.1.call-start = ((), (), s32[]{:S(2)}) async-start(), calls=%async_computation.17 | async-start | bytes 3932160 | tf_op jit(solution)/shard_map/reduce_scatter | solution.py:226
  471.8 16.0 %slice-start.18 = ((s8[6291456]{0:T(1024)(128)(4,1)}), s8[4194304]{0:T(1024)(128)(4,1)S(1)}, s32[]{:S(2)}) async-start(s8[6291456]{0:T(1024)(128)(4,1)} %bitcast.303), calls=%async_computation.37 | async-start | bytes 8388608
  477.5 10.3 slice-start.19
  519.5 10.3 copy-start.49
  533.9 683.4 %all-gather.21.cloned.1.call-start = ((), (), s32[]{:S(2)}) async-start(), calls=%async_computation.18 | async-start | bytes 14665728 | tf_op jit(solution)/shard_map/all_gather | solution.py:272
  586.5 11.2 slice-start.15
  588.1 9.6 slice-start.16
  588.1 9.6 slice-start.17
  603.5 13.0 copy-start.16
  1094.6 7.7 collective-permute-start
  1109.8 16.9 %slice-start.20 = ((s8[6291456]{0:T(1024)(128)(4,1)}), s8[4194304]{0:T(1024)(128)(4,1)S(1)}, s32[]{:S(2)}) async-start(s8[6291456]{0:T(1024)(128)(4,1)} %bitcast.330), calls=%async_computation.39 | async-start | bytes 8388608
  1109.8 16.9 %slice-start.24 = ((s8[4718592]{0:T(1024)(128)(4,1)}), s8[4194304]{0:T(1024)(128)(4,1)S(1)}, s32[]{:S(2)}) async-start(s8[4718592]{0:T(1024)(128)(4,1)} %bitcast.346), calls=%async_computation.43 | async-start | bytes 8388608
  1397.2 25.9 %copy-start.83 = (f32[24,32]{0,1:T(8,128)S(1)}, f32[24,32]{0,1:T(8,128)}, u32[]{:S(2)}) copy-start(f32[24,32]{0,1:T(8,128)} %get-tuple-element.92) | copy-start | bytes 9220
  1397.2 26.6 %copy-start.82 = (f32[24,32]{0,1:T(8,128)S(1)}, f32[24,32]{0,1:T(8,128)}, u32[]{:S(2)}) copy-start(f32[24,32]{0,1:T(8,128)} %get-tuple-element.91) | copy-start | bytes 9220
  (106 other events, 489.7 us)
Sparse Core Ops, SparseCore 0:
  14.9 31.0 all-gather.18
  48.1 28.5 all-gather.16
  78.8 28.5 all-gather.14
  109.3 28.5 all-gather.12
  139.3 28.5 all-gather.10
  169.3 28.5 all-gather.8
  297.7 37.6 reduce-scatter.12
  338.1 37.9 reduce-scatter.8
  378.6 37.9 reduce-scatter.16
  419.1 37.9 reduce-scatter.14
  459.6 37.9 reduce-scatter.10
  534.0 38.3 reduce-scatter.18
  1109.9 107.3 all-gather.20
where the time goes:
time: 1450 us; the launch traced here: 1430 us
  local copies, waits for them, and re-layouts  589 us (41%)
  matrix products  328 us (23%)
  blocking collectives  306 us (21%)
  waiting for transfers between devices  117 us (8%)
  other arithmetic  71.2 us (5%)
  between operations  15.7 us (1%)
    unnamed x1, blocking collectives  306 us
    unnamed x291, local copies, waits for them, and re-layouts  102 us
    reshape x2, local copies, waits for them, and re-layouts, per_device(): flat_grads = flat_grads.reshape(share_len, devices).T.reshape(-1, 128)  93.9 us
    slice x15, local copies, waits for them, and re-layouts, per_device(): summed_all[offset_now:offset_now + piece_count].reshape(grad_piece.shape)  91 us
    reshape x7, local copies, waits for them, and re-layouts, per_device(): summed_all[offset_now:offset_now + piece_count].reshape(grad_piece.shape)  83.3 us
    dot_general x18, matrix products, outer_sum(): jnp.einsum('rtd,rte->de', left_rows, right_rows, preferred_element_type=j...  80.3 us
    all_gather x1, waiting for transfers between devices, per_device(): lax.all_gather(grad_share.astype(jnp.bfloat16), ('rows', 'seq'), axis=0,...  80.1 us
    transpose x1, local copies, waits for them, and re-layouts, per_device(): flat_grads = flat_grads.reshape(share_len, devices).T.reshape(-1, 128)  66.8 us
  transfers between devices with their start and end apart: 14, of which 4 were waited for; matrix products, arithmetic and copies ran while one was open for 30% of the time, Pallas kernels for 0%

commit v1 on v0

--- a/solution.py
+++ b/solution.py
@@ -22,7 +22,10 @@
 
 
 def segment_ids(seg_lengths, row_len):
-    ends = jnp.cumsum(seg_lengths, axis=1)
+    order = jnp.arange(seg_lengths.shape[1])
+    ends = jnp.sum(
+        jnp.where(order[None, :, None] <= order[None, None, :], seg_lengths[:, :, None], 0), axis=1
+    )
     positions = jnp.arange(row_len, dtype=jnp.int32)
     return jnp.sum((positions[None, :, None] >= ends[:, None, :]).astype(jnp.int32), axis=2)
 

time: 1450 us -> 1450 us (level)
    unnamed x291 -> x293, local copies, waits for them, and re-layouts: 102 us -> 103 us
where the time goes in v1:
time: 1450 us; the launch traced here: 1430 us
  local copies, waits for them, and re-layouts  589 us (41%)
  matrix products  328 us (23%)
  blocking collectives  306 us (21%)
  waiting for transfers between devices  117 us (8%)
  other arithmetic  71.8 us (5%)
  between operations  15.7 us (1%)
    unnamed x1, blocking collectives  306 us
    unnamed x293, local copies, waits for them, and re-layouts  103 us
    reshape x2, local copies, waits for them, and re-layouts, per_device(): flat_grads = flat_grads.reshape(share_len, devices).T.reshape(-1, 128)  93.8 us
    slice x15, local copies, waits for them, and re-layouts, per_device(): summed_all[offset_now:offset_now + piece_count].reshape(grad_piece.shape)  91 us
    reshape x7, local copies, waits for them, and re-layouts, per_device(): summed_all[offset_now:offset_now + piece_count].reshape(grad_piece.shape)  83.3 us
    dot_general x18, matrix products, outer_sum(): jnp.einsum('rtd,rte->de', left_rows, right_rows, preferred_element_type=j...  80.2 us
    all_gather x1, waiting for transfers between devices, per_device(): lax.all_gather(grad_share.astype(jnp.bfloat16), ('rows', 'seq'), axis=0,...  80.1 us
    transpose x1, local copies, waits for them, and re-layouts, per_device(): flat_grads = flat_grads.reshape(share_len, devices).T.reshape(-1, 128)  66.8 us
  transfers between devices with their start and end apart: 14, of which 4 were waited for; matrix products, arithmetic and copies ran while one was open for 30% of the time, Pallas kernels for 0%

profile of v1, /device:TPU:1, one launch (start us, length us, event | category | flops | bytes accessed | tf_op | source)
XLA Modules:
  0.0 1432.1 jit_solution(6429721187830957486)
XLA Ops:
  36.2 37.5 %copy.302 = pred[32,128,512]{2,0,1:T(32,128)(4,1)S(1)} copy(pred[32,128,512]{1,0,2:T(32,128)(4,1)S(1)} %iota_compare_fusion) | data formatting | bytes 4194304 | tf_op jit(solution)/shard_map/eq | solution.py:117
  115.3 8.4 fusion.131
  131.2 10.9 fusion.227
  147.4 20.5 %all-gather.11.cloned.1.call-done = bf16[4,512,768]{2,1,0:T(8,128)(2,1)} async-done(((bf16[4,128,768]{2,1,0:T(8,128)(2,1)}), bf16[4,512,768]{2,1,0:T(8,128)(2,1)}) %all-gather.11.cloned.1.call-update) | async-done | bytes 3145744 | tf_op jit(solution)/shard_map/all_gather | solution.py:151
  172.6 8.1 fusion.2
  207.4 7.7 fusion.133
  221.6 9.0 fusion.52
  250.0 7.1 fusion.38
  267.6 12.5 multiply_reduce_fusion.1
  280.8 8.7 convert_reduce_fusion.1
  304.4 15.4 %multiply_reduce_fusion.2 = (f32[4,12,128]{2,1,0:T(8,128)S(1)}, f32[4,12,128,512]{3,2,1,0:T(8,128)}) fusion(f32[4,12,128,512]{3,2,1,0:T(8,128)} %copy-done.3, f32[4,12,128]{2,1,0:T(8,128)S(1)} %log_add_fusion.2, bf16[4,128,12,64]{1,3,2,0:T(8,128)(2,1)} %bitcast.326, bf16[4,512,12,64]{1,3,2,0:T(8,128)(2,1)} %bitcast.311), kind=kOutput, calls=%fused_computation.11 | convolution fusion | flops 412084224 | bytes 29147136 | tf_op jit(solution)/shard_map/rqhd,rkhd->rhqk/dot_general | solution.py:200
  319.8 8.6 convert_reduce_fusion.2
  342.3 13.3 multiply_reduce_fusion
  357.9 8.6 convert_reduce_fusion
  375.5 7.1 fusion.89
  388.5 7.2 fusion.86
  400.4 7.1 fusion.92
  442.7 7.3 fusion.190
  456.7 9.4 fusion.7
  477.8 10.2 fusion.168
  488.0 9.0 bitcast_add_fusion
  497.1 10.7 reshape.418
  507.8 6.7 add_add_fusion
  559.9 12.6 reduce-scatter.19.cloned.1.call-done
  588.2 9.6 constant_dynamic-update-slice_fusion.4
  607.7 6.8 fusion.124
  616.7 9.9 pad.4
  626.7 66.6 %reshape.420 = f32[221312,32]{1,0:T(8,128)} reshape(f32[7081984]{0:T(1024)} %pad.4) | data formatting | bytes 56655872 | tf_op jit(solution)/shard_map/reshape | solution.py:270
  693.2 66.8 %copy.345 = f32[32,221312]{1,0:T(8,128)} copy(f32[32,221312]{0,1:T(8,128)} %bitcast.69) | data formatting | bytes 56655872 | tf_op jit(solution)/shard_map/transpose | solution.py:270
  760.1 27.3 %reshape.421 = f32[55328,128]{1,0:T(8,128)} reshape(f32[32,221312]{1,0:T(8,128)} %copy.345) | data formatting | bytes 56655872 | tf_op jit(solution)/shard_map/reshape | solution.py:270
  787.4 305.7 %fusion = f32[1744,128]{1,0:T(8,128)} fusion(f32[55328,128]{1,0:T(8,128)} %reshape.421), kind=kCustom, calls=%all-reduce-scatter | all-reduce-scatter fusion | flops 7143425 | bytes 29220864
  1109.9 8.5 add_convert_fusion
  1118.4 8.3 add_convert_fusion.1
  1137.2 80.1 %all-gather.21.cloned.1.call-done = bf16[32,1729,128]{2,1,0:T(8,128)(2,1)} async-done(((bf16[1,1729,128]{2,1,0:T(8,128)(2,1)}), bf16[32,1729,128]{2,1,0:T(8,128)(2,1)}) %all-gather.21.cloned.1.call-update) | async-done | bytes 14163984 | tf_op jit(solution)/shard_map/all_gather | solution.py:275
  1217.4 33.1 %copy.385 = f32[4,8,1729,128]{3,1,2,0:T(8,128)} copy(bf16[4,8,1729,128]{3,2,1,0:T(8,128)(2,1)} %bitcast.305) | data formatting | bytes 42491904
  1250.4 6.9 fusion.224
  1257.3 13.4 fusion.223
  1272.9 6.7 copy.346
  1279.6 7.4 reshape.423
  1287.0 6.7 copy.347
  1293.7 7.4 reshape.424
  1301.2 6.7 copy.348
  1307.9 7.4 reshape.425
  1320.3 7.4 reshape.426
  1327.7 20.9 %copy.350 = f32[73728,32]{1,0:T(8,128)} copy(f32[73728,32]{0,1:T(8,128)} %get-tuple-element.94) | data formatting | bytes 18874368 | tf_op jit(solution)/shard_map/slice | solution.py:283
  1348.6 27.7 %reshape.427 = f32[768,3072]{1,0:T(8,128)} reshape(f32[73728,32]{1,0:T(8,128)} %copy.350) | data formatting | bytes 18874368 | tf_op jit(solution)/shard_map/reshape | solution.py:283
  1376.3 20.9 %copy.351 = f32[73728,32]{1,0:T(8,128)} copy(f32[73728,32]{0,1:T(8,128)} %get-tuple-element.93) | data formatting | bytes 18874368 | tf_op jit(solution)/shard_map/slice | solution.py:283
  1397.2 25.9 %reshape.428 = f32[3072,768]{1,0:T(8,128)} reshape(f32[73728,32]{1,0:T(8,128)} %copy.351) | data formatting | bytes 18874368 | tf_op jit(solution)/shard_map/reshape | solution.py:283
  (471 shorter events, 364.9 us)
Async XLA Ops:
  7.2 84.4 %all-gather.19.cloned.1.call-start = ((), (), s32[]{:S(2)}) async-start(), calls=%async_computation.11 | async-start | bytes 3932160 | tf_op jit(solution)/shard_map/all_gather | solution.py:151
  10.9 22.1 %copy-start.79 = (f32[768]{0:T(1024)}, f32[768]{0:T(1024)S(1)}, u32[]{:S(2)}) copy-start(f32[768]{0:T(1024)S(1)} %convert_element_type.340) | copy-start | bytes 9220
  11.5 16.8 %copy-start.84 = (f32[4,128]{1,0:T(4,128)}, f32[4,128]{1,0:T(4,128)S(1)}, u32[]{:S(2)}) copy-start(f32[4,128]{1,0:T(4,128)S(1)} %get-tuple-element.117) | copy-start | bytes 6148
  11.5 19.8 %copy-start.90 = (f32[4,128]{1,0:T(4,128)}, f32[4,128]{1,0:T(4,128)S(1)}, u32[]{:S(2)}) copy-start(f32[4,128]{1,0:T(4,128)S(1)} %get-tuple-element.144) | copy-start | bytes 6148
  14.7 95.9 %all-gather.17.cloned.1.call-start = ((), (), s32[]{:S(2)}) async-start(), calls=%async_computation.10 | async-start | bytes 3932160 | tf_op jit(solution)/shard_map/all_gather | solution.py:152
  16.5 110.0 %all-gather.15.cloned.1.call-start = ((), (), s32[]{:S(2)}) async-start(), calls=%async_computation.9 | async-start | bytes 3932160 | tf_op jit(solution)/shard_map/all_gather | solution.py:151
  19.6 123.1 %all-gather.13.cloned.1.call-start = ((), (), s32[]{:S(2)}) async-start(), calls=%async_computation.8 | async-start | bytes 3932160 | tf_op jit(solution)/shard_map/all_gather | solution.py:152
  21.4 146.5 %all-gather.11.cloned.1.call-start = ((), (), s32[]{:S(2)}) async-start(), calls=%async_computation.7 | async-start | bytes 3932160 | tf_op jit(solution)/shard_map/all_gather | solution.py:151
  22.7 10.3 copy-start.87
  25.8 177.0 %all-gather.9.cloned.1.call-start = ((), (), s32[]{:S(2)}) async-start(), calls=%async_computation.6 | async-start | bytes 3932160 | tf_op jit(solution)/shard_map/all_gather | solution.py:152
  27.6 510.0 %reduce-scatter.13.cloned.1.call-start = ((), (), s32[]{:S(2)}) async-start(), calls=%async_computation.14 | async-start | bytes 3932160 | tf_op jit(solution)/shard_map/reduce_scatter | solution.py:226
  35.0 38.7 %copy-start.103 = (bf16[32,12]{0,1:T(8,128)(2,1)S(1)}, bf16[32,12]{0,1:T(8,128)(2,1)}, u32[]{:S(2)}) copy-start(bf16[32,12]{0,1:T(8,128)(2,1)} %param.22) | copy-start | bytes 2308
  216.1 44.9 %copy-start.20 = (f32[4,128,768]{2,1,0:T(8,128)}, f32[4,128,768]{2,1,0:T(8,128)S(1)}, u32[]{:S(2)}) copy-start(f32[4,128,768]{2,1,0:T(8,128)S(1)} %get-tuple-element.135) | copy-start | bytes 4718596
  216.8 13.9 slice-start.13
  216.9 19.2 %slice-start.22 = ((s8[4718592]{0:T(1024)(128)(4,1)}), s8[4194304]{0:T(1024)(128)(4,1)S(1)}, s32[]{:S(2)}) async-start(s8[4718592]{0:T(1024)(128)(4,1)} %bitcast.344), calls=%async_computation.41 | async-start | bytes 8388608
  221.6 14.5 %slice-start.23 = ((s8[4718592]{0:T(1024)(128)(4,1)}), s8[524288]{0:T(1024)(128)(4,1)S(1)}, s32[]{:S(2)}) async-start(s8[4718592]{0:T(1024)(128)(4,1)} %bitcast.344), calls=%async_computation.42 | async-start | bytes 1048576
  263.2 73.7 %copy-start.24 = (f32[4,128,768]{2,1,0:T(8,128)}, f32[4,128,768]{2,1,0:T(8,128)S(1)}, u32[]{:S(2)}) copy-start(f32[4,128,768]{2,1,0:T(8,128)S(1)} %get-tuple-element.104) | copy-start | bytes 4718596
  267.6 12.5 slice-start.3
  267.6 12.5 slice-start.4
  267.6 13.2 slice-start.5
  267.6 13.2 copy-start.70
  297.8 243.3 %reduce-scatter.9.cloned.1.call-start = ((), (), s32[]{:S(2)}) async-start(), calls=%async_computation.12 | async-start | bytes 3932160 | tf_op jit(solution)/shard_map/reduce_scatter | solution.py:226
  304.3 15.5 %copy-start.72 = (f32[4,12,128]{2,1,0:T(8,128)}, f32[4,12,128]{2,1,0:T(8,128)S(1)}, u32[]{:S(2)}) copy-start(f32[4,12,128]{2,1,0:T(8,128)S(1)} %log_add_fusion.2) | copy-start | bytes 73732
  304.3 15.4 %slice-start.6 = ((s8[12582912]{0:T(1024)(128)(4,1)}), s8[4194304]{0:T(1024)(128)(4,1)S(1)}, s32[]{:S(2)}) async-start(s8[12582912]{0:T(1024)(128)(4,1)} %bitcast.282), calls=%async_computation.25 | async-start | bytes 8388608
  304.3 15.4 %slice-start.7 = ((s8[12582912]{0:T(1024)(128)(4,1)}), s8[4194304]{0:T(1024)(128)(4,1)S(1)}, s32[]{:S(2)}) async-start(s8[12582912]{0:T(1024)(128)(4,1)} %bitcast.282), calls=%async_computation.26 | async-start | bytes 8388608
  304.4 15.4 %slice-start.8 = ((s8[12582912]{0:T(1024)(128)(4,1)}), s8[4194304]{0:T(1024)(128)(4,1)S(1)}, s32[]{:S(2)}) async-start(s8[12582912]{0:T(1024)(128)(4,1)} %bitcast.282), calls=%async_computation.27 | async-start | bytes 8388608
  336.7 207.8 %reduce-scatter.17.cloned.1.call-start = ((), (), s32[]{:S(2)}) async-start(), calls=%async_computation.16 | async-start | bytes 3932160 | tf_op jit(solution)/shard_map/reduce_scatter | solution.py:226
  342.2 13.4 copy-start.74
  342.2 13.4 slice-start
  342.2 13.4 slice-start.1
  342.3 15.6 %slice-start.2 = ((s8[12582912]{0:T(1024)(128)(4,1)}), s8[4194304]{0:T(1024)(128)(4,1)S(1)}, s32[]{:S(2)}) async-start(s8[12582912]{0:T(1024)(128)(4,1)} %bitcast.278), calls=%async_computation.21 | async-start | bytes 8388608
  374.8 178.2 %reduce-scatter.15.cloned.1.call-start = ((), (), s32[]{:S(2)}) async-start(), calls=%async_computation.15 | async-start | bytes 3932160 | tf_op jit(solution)/shard_map/reduce_scatter | solution.py:229
  387.3 169.2 %reduce-scatter.11.cloned.1.call-start = ((), (), s32[]{:S(2)}) async-start(), calls=%async_computation.13 | async-start | bytes 3932160 | tf_op jit(solution)/shard_map/reduce_scatter | solution.py:229
  407.6 12.9 slice-start.9
  455.3 117.2 %reduce-scatter.19.cloned.1.call-start = ((), (), s32[]{:S(2)}) async-start(), calls=%async_computation.17 | async-start | bytes 3932160 | tf_op jit(solution)/shard_map/reduce_scatter | solution.py:229
  472.1 16.0 %slice-start.18 = ((s8[6291456]{0:T(1024)(128)(4,1)}), s8[4194304]{0:T(1024)(128)(4,1)S(1)}, s32[]{:S(2)}) async-start(s8[6291456]{0:T(1024)(128)(4,1)} %bitcast.303), calls=%async_computation.37 | async-start | bytes 8388608
  477.8 10.2 slice-start.19
  519.7 10.3 copy-start.49
  534.2 683.2 %all-gather.21.cloned.1.call-start = ((), (), s32[]{:S(2)}) async-start(), calls=%async_computation.18 | async-start | bytes 14665728 | tf_op jit(solution)/shard_map/all_gather | solution.py:275
  586.6 11.2 slice-start.15
  588.2 9.6 slice-start.16
  588.2 9.6 slice-start.17
  603.7 13.0 copy-start.16
  1094.7 7.7 collective-permute-start
  1109.9 16.9 %slice-start.20 = ((s8[6291456]{0:T(1024)(128)(4,1)}), s8[4194304]{0:T(1024)(128)(4,1)S(1)}, s32[]{:S(2)}) async-start(s8[6291456]{0:T(1024)(128)(4,1)} %bitcast.330), calls=%async_computation.39 | async-start | bytes 8388608
  1109.9 16.9 %slice-start.24 = ((s8[4718592]{0:T(1024)(128)(4,1)}), s8[4194304]{0:T(1024)(128)(4,1)S(1)}, s32[]{:S(2)}) async-start(s8[4718592]{0:T(1024)(128)(4,1)} %bitcast.346), calls=%async_computation.43 | async-start | bytes 8388608
  1397.2 25.9 %copy-start.83 = (f32[24,32]{0,1:T(8,128)S(1)}, f32[24,32]{0,1:T(8,128)}, u32[]{:S(2)}) copy-start(f32[24,32]{0,1:T(8,128)} %get-tuple-element.92) | copy-start | bytes 9220
  1397.2 26.6 %copy-start.82 = (f32[24,32]{0,1:T(8,128)S(1)}, f32[24,32]{0,1:T(8,128)}, u32[]{:S(2)}) copy-start(f32[24,32]{0,1:T(8,128)} %get-tuple-element.91) | copy-start | bytes 9220
  (107 other events, 496.3 us)
Sparse Core Ops, SparseCore 0:
  14.8 31.0 all-gather.18
  48.0 28.5 all-gather.16
  78.8 28.5 all-gather.14
  109.4 28.5 all-gather.12
  139.4 28.5 all-gather.10
  169.3 28.5 all-gather.8
  297.9 37.5 reduce-scatter.12
  338.2 37.9 reduce-scatter.8
  378.7 37.9 reduce-scatter.16
  419.2 37.9 reduce-scatter.14
  459.8 37.9 reduce-scatter.10
  534.3 38.2 reduce-scatter.18
  1110.0 107.3 all-gather.20

commit v2 on v1

v2 whole, which is shorter than its diff:
```python
import functools
import math

import jax
import jax.numpy as jnp
from jax import lax
from jax.experimental import pallas as pl
from jax.experimental.pallas import tpu as pltpu
from jax.sharding import PartitionSpec as P

EPSILON = 1e-06
THRESHOLDS = (12, 16, 23, 32, 46, 64, 91)
NEGATIVE = -1e30
GELU_SCALE = math.sqrt(2.0 / math.pi)
GELU_CUBIC = 0.044715
LOG2E = math.log2(math.e)
BLK = 128
QT = 256
HALF = 64
ONES_AT = 8
BF = jnp.bfloat16
F32 = jnp.float32
MESH = pl.DeviceIdType.MESH
CH = 256
LAG = 2


def bucket_of(offsets, bucket_count):
    distance = jnp.abs(offsets)
    levels = 8 + sum(((distance >= threshold).astype(jnp.int32) for threshold in THRESHOLDS))
    return jnp.where(offsets > 0, bucket_count // 2, 0) + jnp.where(distance < 8, distance, levels)


def segment_ids(seg_lengths, row_len):
    order = jnp.arange(seg_lengths.shape[1])
    ends = jnp.sum(
        jnp.where(order[None, :, None] <= order[None, None, :], seg_lengths[:, :, None], 0), axis=1
    )
    positions = jnp.arange(row_len, dtype=jnp.int32)
    return jnp.sum((positions[None, :, None] >= ends[:, None, :]).astype(jnp.int32), axis=2)


def gelu_slope(values_in):
    tangent = jnp.tanh(GELU_SCALE * (values_in + GELU_CUBIC * values_in * values_in * values_in))
    return 0.5 * (1.0 + tangent) + 0.5 * values_in * (1.0 - tangent * tangent) * GELU_SCALE * (
        1.0 + 3.0 * GELU_CUBIC * values_in * values_in
    )


def apply_rms_scaling(values_in, gain_row):
    inverse = lax.rsqrt(jnp.mean(values_in * values_in, axis=-1, keepdims=True) + EPSILON)
    return (values_in * inverse * gain_row, inverse)


def norm_back(values_in, inverse, gain_row, grad_normed):
    weighted = grad_normed * gain_row
    inner_mean = jnp.mean(weighted * values_in, axis=-1, keepdims=True)
    grad_values = inverse * weighted - values_in * (inverse * inverse * inverse) * inner_mean
    grad_gain = jnp.sum(grad_normed * values_in * inverse, axis=0)
    return (grad_values, grad_gain)


def dot(a, b, ca, cb):
    return lax.dot_general(a, b, (((ca,), (cb,)), ((), ())), preferred_element_type=F32)


def halves(value, own, other, head):
    lane = lax.broadcasted_iota(jnp.int32, value.shape, 1)
    mine = (lane < HALF) if head == 0 else (lane >= HALF)
    return jnp.where(mine, value, other)


def stack_q(q_pair, features, head):
    scaled = q_pair[head * HALF : (head + 1) * HALF].astype(F32) * LOG2E
    high = scaled.astype(BF)
    low = (scaled - high.astype(F32)).astype(BF)
    zero = jnp.zeros_like(high)
    if head == 0:
        return jnp.concatenate([high, zero, low, features], axis=0)
    return jnp.concatenate([zero, high, features, low], axis=0)


def bias_tile(bias_ref, head, key_block, query_tile, blocks):
    at = key_block - query_tile * (QT // BLK) + blocks - 1
    return jnp.concatenate([bias_ref[head, at - i] for i in range(QT // BLK)], axis=1)


def attend_kernel(q_ref, k_ref, v_ref, fq_ref, fk_ref, bias_ref, mix_ref, stat_ref):
    row_len = k_ref.shape[0]
    blocks = row_len // BLK
    keys, features_k = k_ref[...], fk_ref[0]
    v_flat = v_ref[...].T
    for head in range(2):
        q_all = stack_q(q_ref[...], fq_ref[0], head)
        k_all = jnp.concatenate([keys, halves(keys, None, features_k, head)], axis=1)
        v_head = jnp.concatenate(
            [v_flat[head * HALF : (head + 1) * HALF], jnp.ones((16, row_len), BF)], axis=0
        )
        for tile in range(row_len // QT):
            cut = slice(tile * QT, (tile + 1) * QT)
            raw = dot(k_all, q_all[:, cut], 1, 0)
            scores = jnp.concatenate(
                [
                    raw[b * BLK : (b + 1) * BLK] + bias_tile(bias_ref, head, b, tile, blocks)
                    for b in range(blocks)
                ],
                axis=0,
            )
            top = jnp.max(scores, axis=0, keepdims=True)
            probs = jnp.exp2(scores - top).astype(BF)
            summed = dot(v_head, probs, 1, 0)
            total = summed[HALF : HALF + 1]
            mix_ref[head * HALF : (head + 1) * HALF, cut] = (
                summed[:HALF] * (1.0 / total)
            ).astype(BF)
            stat_ref[0, 0, head : head + 1, cut] = top + jnp.log2(total)


def three(row):
    one = row.astype(BF)
    rest = row - one.astype(F32)
    two = rest.astype(BF)
    return one, two, (rest - two.astype(F32)).astype(BF)


def feature_rows(base, row):
    parts = three(row)
    at = lax.broadcasted_iota(jnp.int32, base.shape, 0)
    out = base.astype(F32)
    for i, part in enumerate(parts):
        out = jnp.where(at == ONES_AT + i, part.astype(F32), out)
    return out.astype(BF)


def attend_back_kernel(
    q_ref, k_ref, v_ref, do_ref, mix_ref, stat_ref, fq_ref, fk_ref, bias_ref,
    dq_ref, dk_ref, dv_ref, acc_ref, dk_sum, dv_sum,
):
    row_len = k_ref.shape[0]
    blocks = row_len // BLK
    keys, vals, features_k = k_ref[...], v_ref[...], fk_ref[0]
    k_flat = keys.T
    q_rows, do_rows = q_ref[...].T, do_ref[...].T
    zero_rows = jnp.zeros((row_len, BLK), BF)

    @pl.when(pl.program_id(1) == 0)
    def _():
        acc_ref[...] = jnp.zeros_like(acc_ref)

    for head in range(2):
        span = slice(head * HALF, (head + 1) * HALF)
        do_head = do_ref[span]
        delta = jnp.sum(do_head.astype(F32) * mix_ref[span].astype(F32), axis=0, keepdims=True)
        zeros = jnp.zeros((HALF, row_len), BF)
        q_all = stack_q(q_ref[...], feature_rows(fq_ref[0], -stat_ref[0, 0, head : head + 1]), head)
        k_all = jnp.concatenate([keys, halves(keys, None, features_k, head)], axis=1)
        v_all = halves(vals, None, features_k, head)
        back = feature_rows(zeros, -delta)
        do_all = jnp.concatenate([do_head, back] if head == 0 else [back, do_head], axis=0)
        q_own = halves(q_rows, None, zero_rows, head)
        do_own = halves(do_rows, None, zero_rows, head)
        for tile in range(row_len // QT):
            cut = slice(tile * QT, (tile + 1) * QT)
            raw = dot(k_all, q_all[:, cut], 1, 0)
            grad_probs = dot(v_all, do_all[:, cut], 1, 0)
            probs_list, grads_list = [], []
            sums = {}
            for b in range(blocks):
                part = slice(b * BLK, (b + 1) * BLK)
                probs = jnp.exp2(raw[part] + bias_tile(bias_ref, head, b, tile, blocks))
                grads = probs * grad_probs[part]
                probs_list.append(probs.astype(BF))
                grads_list.append(grads.astype(BF))
                for i in range(QT // BLK):
                    at = b - tile * (QT // BLK) - i + blocks - 1
                    piece = grads[:, i * BLK : (i + 1) * BLK]
                    sums[at] = sums[at] + piece if at in sums else piece
            for at, piece in sums.items():
                acc_ref[head, at] += piece
            probs_low = jnp.concatenate(probs_list, axis=0)
            grads_low = jnp.concatenate(grads_list, axis=0)
            dv_new = dot(probs_low, do_own[cut], 1, 0)
            dk_new = dot(grads_low, q_own[cut], 1, 0)
            if head == 0 and tile == 0:
                dv_sum[...] = dv_new
                dk_sum[...] = dk_new
            else:
                dv_sum[...] += dv_new
                dk_sum[...] += dk_new
            dq_ref[span, cut] = dot(k_flat[span], grads_low, 1, 0).astype(BF)
    dk_ref[...] = dk_sum[...].astype(BF)
    dv_ref[...] = dv_sum[...].astype(BF)


def specs(row_len):
    flat = pl.BlockSpec((BLK, row_len), lambda g, r: (g, r))
    rows = pl.BlockSpec((row_len, BLK), lambda g, r: (r, g))
    stat = pl.BlockSpec((1, 1, 2, row_len), lambda g, r: (r, g, 0, 0))
    fq = pl.BlockSpec((1, HALF, row_len), lambda g, r: (r, 0, 0))
    fk = pl.BlockSpec((1, row_len, BLK), lambda g, r: (r, 0, 0))
    blocks = 2 * (row_len // BLK) - 1
    bias = pl.BlockSpec((2, blocks, BLK, BLK), lambda g, r: (g, 0, 0, 0))
    return flat, rows, stat, fq, fk, bias


def attend(q_flat, k_rows, v_rows, fq, fk, bias, row_len):
    width, count = q_flat.shape
    flat, rows, stat, fqs, fks, biass = specs(row_len)
    pairs, row_count = width // BLK, count // row_len
    return pl.pallas_call(
        attend_kernel,
        grid=(pairs, row_count),
        in_specs=[flat, rows, rows, fqs, fks, biass],
        out_specs=[flat, stat],
        out_shape=[
            jax.ShapeDtypeStruct((width, count), BF),
            jax.ShapeDtypeStruct((row_count, pairs, 2, row_len), F32),
        ],
        compiler_params=pltpu.CompilerParams(vmem_limit_bytes=48 << 20),
        cost_estimate=pl.CostEstimate(
            flops=4 * 4 * width * count * row_len,
            bytes_accessed=8 * width * count,
            transcendentals=0,
        ),
    )(q_flat, k_rows, v_rows, fq, fk, bias)


def attend_back(q_flat, k_rows, v_rows, do_flat, mix_flat, stat_in, fq, fk, bias, row_len):
    width, count = q_flat.shape
    flat, rows, stat, fqs, fks, biass = specs(row_len)
    pairs, row_count = width // BLK, count // row_len
    return pl.pallas_call(
        attend_back_kernel,
        grid=(pairs, row_count),
        in_specs=[flat, rows, rows, flat, flat, stat, fqs, fks, biass],
        out_specs=[flat, rows, rows, biass],
        out_shape=[
            jax.ShapeDtypeStruct((width, count), BF),
            jax.ShapeDtypeStruct((count, width), BF),
            jax.ShapeDtypeStruct((count, width), BF),
            jax.ShapeDtypeStruct(bias.shape, F32),
        ],
        scratch_shapes=[pltpu.VMEM((row_len, BLK), F32)] * 2,
        compiler_params=pltpu.CompilerParams(vmem_limit_bytes=48 << 20),
        cost_estimate=pl.CostEstimate(
            flops=10 * 4 * width * count * row_len,
            bytes_accessed=16 * width * count,
            transcendentals=0,
        ),
    )(q_flat, k_rows, v_rows, do_flat, mix_flat, stat_in, fq, fk, bias)


class Place:
    def __init__(self):
        self.r, self.s = lax.axis_index("rows"), lax.axis_index("seq")
        self.x, self.z = lax.rem(self.r, 2), self.r // 2
        self.core, self.y = lax.rem(self.s, 2), self.s // 2

    def at(self, x=None, y=None, core=None, z=None):
        x = self.x if x is None else x
        y = self.y if y is None else y
        core = self.core if core is None else core
        z = self.z if z is None else z
        return (z * 2 + x, y * 2 + core)


def reduce_kernel(chunks, depth, scale, in_ref, out_ref, got, own, got_one, got_two, got_z, share,
                  load_sem, keep_sem, send, recv, send_z, recv_z):
    me = Place()
    w = in_ref.shape[1] // 2
    half, quarter, piece = CH // 2, CH // 4, CH // (4 * depth)
    barrier = pltpu.get_barrier_semaphore()
    others = [me.at(core=1 - me.core), me.at(x=1 - me.x), me.at(y=1 - me.y)]
    others += [me.at(z=lax.rem(me.z + k, depth)) for k in range(1, depth)]
    for place in others:
        pl.semaphore_signal(barrier, inc=1, device_id=place, device_id_type=MESH)
    pl.semaphore_wait(barrier, len(others))

    def copy(src, dst, stage, c, place):
        return pltpu.make_async_remote_copy(
            src_ref=src, dst_ref=dst, send_sem=send.at[stage, c], recv_sem=recv.at[stage, c],
            device_id=place, device_id_type=MESH)

    def lanes(core):
        return pl.ds(pl.multiple_of(core * w, 128), w)

    def rows(base, size):
        return pl.ds(pl.multiple_of(base, 16), size)

    def order(c):
        odd = lax.rem(c, 2)
        one = jnp.where(odd == 0, me.x, me.y)
        two = jnp.where(odd == 0, me.y, me.x)
        x_first = (me.r + (1 - odd) * (1 - 2 * me.x), me.s + odd * (2 - 4 * me.y))
        y_first = (me.r + odd * (1 - 2 * me.x), me.s + (1 - odd) * (2 - 4 * me.y))
        return one, two, x_first, y_first

    def load(c):
        return pltpu.make_async_copy(in_ref.at[rows(c * CH, CH), lanes(me.core)], own.at[c], load_sem.at[c])

    def step_core(c):
        return copy(in_ref.at[rows(c * CH, CH), lanes(1 - me.core)], got.at[c], 0, c, me.at(core=1 - me.core))

    def step_one(c):
        one, _, place, _ = order(c)
        return copy(own.at[c, rows((1 - one) * half, half)], got_one.at[c], 1, c, place)

    def step_two(c):
        one, two, _, place = order(c)
        return copy(own.at[c, rows(one * half + (1 - two) * quarter, quarter)], got_two.at[c], 2, c, place)

    def base(c):
        one, two, _, _ = order(c)
        return one * half + two * quarter

    def step_z(c, k):
        to = lax.rem(me.z + k, depth)
        return pltpu.make_async_remote_copy(
            src_ref=own.at[c, rows(base(c) + to * piece, piece)], dst_ref=got_z.at[c, depth - 1 - k],
            send_sem=send_z.at[0, c, k - 1], recv_sem=recv_z.at[0, c, depth - 1 - k],
            device_id=me.at(z=to), device_id_type=MESH)

    def keep(c):
        return pltpu.make_async_copy(
            share.at[c], out_ref.at[rows(c * CH + base(c) + me.z * piece, piece), lanes(me.core)], keep_sem.at[c])

    def give_z(c, k):
        to = lax.rem(me.z + k, depth)
        return pltpu.make_async_remote_copy(
            src_ref=share.at[c],
            dst_ref=out_ref.at[rows(c * CH + base(c) + me.z * piece, piece), lanes(me.core)],
            send_sem=send_z.at[1, c, k - 1], recv_sem=recv_z.at[1, c, depth - 1 - k],
            device_id=me.at(z=to), device_id_type=MESH)

    def give_two(c):
        one, two, _, place = order(c)
        part = out_ref.at[rows(c * CH + one * half + two * quarter, quarter), lanes(me.core)]
        return copy(part, part, 3, c, place)

    def give_one(c):
        one, _, place, _ = order(c)
        part = out_ref.at[rows(c * CH + one * half, half), lanes(me.core)]
        return copy(part, part, 4, c, place)

    def give_core(c):
        part = out_ref.at[rows(c * CH, CH), lanes(me.core)]
        return copy(part, part, 5, c, me.at(core=1 - me.core))

    def add(c, start, size, from_ref):
        part = rows(start, size)
        own[c, part] = (own[c, part].astype(F32) + from_ref[c].astype(F32)).astype(BF)

    def run(stage, c):
        if stage == 0:
            step_core(c).start()
        if stage == 1:
            step_core(c).wait_recv()
            load(c).wait()
            add(c, 0, CH, got)
            step_one(c).start()
        if stage == 2:
            step_one(c).wait_recv()
            one, _, _, _ = order(c)
            add(c, one * half, half, got_one)
            step_two(c).start()
        if stage == 3:
            step_two(c).wait_recv()
            add(c, base(c), quarter, got_two)
            for k in range(1, depth):
                step_z(c, k).start()
        if stage == 4:
            for k in range(1, depth):
                step_z(c, k).wait_recv()
            total = own[c, rows(base(c) + me.z * piece, piece)].astype(F32)
            for k in range(depth - 1):
                total = total + got_z[c, k].astype(F32)
            share[c] = (total * scale).astype(BF)
            keep(c).start()
            for k in range(1, depth):
                give_z(c, k).start()
        if stage == 5:
            keep(c).wait()
            for k in range(1, depth):
                give_z(c, k).wait_recv()
            give_two(c).start()
        if stage == 6:
            give_two(c).wait_recv()
            give_one(c).start()
        if stage == 7:
            give_one(c).wait_recv()
            give_core(c).start()
        if stage == 8:
            give_core(c).wait_recv()
            for d in (step_core(c), step_one(c), step_two(c), give_two(c), give_one(c), give_core(c)):
                d.wait_send()
            for k in range(1, depth):
                step_z(c, k).wait_send()
                give_z(c, k).wait_send()

    def first(c, _):
        load(c).start()
        return 0

    lax.fori_loop(0, chunks, first, 0)

    def tick(t, _):
        for stage in range(8, -1, -1):
            p = t - stage * LAG

            @pl.when((p >= 0) & (p < chunks // 2))
            def _():
                run(stage, 2 * p)
                run(stage, 2 * p + 1)
        return 0

    lax.fori_loop(0, chunks // 2 + 8 * LAG, tick, 0)


def reduce_ring(flat, scale, depth):
    chunks, w = flat.shape[0] // CH, flat.shape[1] // 2
    piece = CH // (4 * depth)
    dma = pltpu.SemaphoreType.DMA
    return pl.pallas_call(
        functools.partial(reduce_kernel, chunks, depth, scale),
        out_shape=jax.ShapeDtypeStruct(flat.shape, BF),
        in_specs=[pl.BlockSpec(memory_space=pl.ANY)],
        out_specs=pl.BlockSpec(memory_space=pl.ANY),
        scratch_shapes=[
            pltpu.VMEM((chunks, CH, w), BF),
            pltpu.VMEM((chunks, CH, w), BF),
            pltpu.VMEM((chunks, CH // 2, w), BF),
            pltpu.VMEM((chunks, CH // 4, w), BF),
            pltpu.VMEM((chunks, depth - 1, piece, w), BF),
            pltpu.VMEM((chunks, piece, w), BF),
            dma((chunks,)), dma((chunks,)),
            dma((6, chunks)), dma((6, chunks)),
            dma((2, chunks, depth - 1)), dma((2, chunks, depth - 1)),
        ],
        compiler_params=pltpu.CompilerParams(
            collective_id=0, has_side_effects=True, vmem_limit_bytes=56 << 20),
    )(flat)


def reduce_plain(flat, scale):
    share = lax.psum_scatter(flat, ("rows", "seq"), scatter_dimension=0, tiled=True)
    share = (share.astype(F32) * scale).astype(BF)
    return lax.all_gather(share, ("rows", "seq"), axis=0, tiled=True)


def reduce_all(flat, scale):
    depth = lax.axis_size("rows") // 2
    if lax.axis_size("seq") == 4 and CH % (4 * depth * 16) == 0:
        return reduce_ring(flat, scale, depth)
    return reduce_plain(flat, scale)


def per_device(
    tokens, seg_lengths, w_query, w_key, w_value, w_output, w_inner, w_outer,
    gain_attn, gain_ffn, bucket_bias_table, cotangent,
):
    rows_dev, piece_len, width = tokens.shape
    seq_parts = lax.axis_size("seq")
    row_len = piece_len * seq_parts
    bucket_count, head_count = bucket_bias_table.shape
    mine = rows_dev // seq_parts
    count = mine * row_len
    seg_count = seg_lengths.shape[1]
    gain_one = gain_attn.astype(F32)
    gain_two = gain_ffn.astype(F32)

    def to_rows(array_in):
        out = lax.all_to_all(array_in, "seq", split_axis=0, concat_axis=1, tiled=True)
        return out.reshape(count, width)

    def from_rows(array_in):
        return lax.all_to_all(
            array_in.reshape(mine, row_len, width), "seq", split_axis=1, concat_axis=0, tiled=True
        )

    lengths = lax.dynamic_slice_in_dim(seg_lengths, lax.axis_index("seq") * mine, mine, 0)
    seg = segment_ids(lengths, row_len)
    slots = jnp.arange(HALF, dtype=jnp.int32)
    fq = (seg[:, None, :] == slots[None, :, None]).astype(BF)
    fk_half = jnp.where(
        slots < seg_count,
        jnp.where(seg[:, :, None] != slots, NEGATIVE, 0.0),
        jnp.where((slots >= ONES_AT) & (slots < ONES_AT + 3), 1.0, 0.0),
    ).astype(BF)
    fk = jnp.concatenate([fk_half, fk_half], axis=2)
    blocks = row_len // BLK
    offsets = (
        (jnp.arange(2 * blocks - 1, dtype=jnp.int32) - (blocks - 1))[:, None, None] * BLK
        + jnp.arange(BLK, dtype=jnp.int32)[None, :, None]
        - jnp.arange(BLK, dtype=jnp.int32)[None, None, :]
    )
    buckets = bucket_of(offsets, bucket_count)
    indicator = (
        buckets[None] == jnp.arange(bucket_count, dtype=jnp.int32)[:, None, None, None]
    ).astype(BF)
    bias = (
        jnp.einsum("zbfu,zi->ibfu", indicator, bucket_bias_table, preferred_element_type=F32)
        * LOG2E
    )

    tok = to_rows(tokens)
    grad_out = to_rows(cotangent)
    wide = tok.astype(F32)
    normed_wide, inverse_one = apply_rms_scaling(wide, gain_one)
    normed = normed_wide.astype(BF)
    q_flat = dot(w_query, normed, 0, 1).astype(BF)
    k_rows = dot(normed, w_key, 1, 0).astype(BF)
    v_rows = dot(normed, w_value, 1, 0).astype(BF)
    mix_flat, stat = attend(q_flat, k_rows, v_rows, fq, fk, bias, row_len)
    hidden = wide + dot(mix_flat, w_output, 0, 0)
    normed_two_wide, inverse_two = apply_rms_scaling(hidden, gain_two)
    normed_two = normed_two_wide.astype(BF)
    inner_pre = dot(normed_two, w_inner, 1, 0)
    active = jax.nn.gelu(inner_pre, approximate=True).astype(BF)
    result = (hidden + dot(active, w_outer, 1, 0)).astype(BF)
    grad_pre = (dot(grad_out, w_outer, 1, 1) * gelu_slope(inner_pre)).astype(BF)
    sum_outer = dot(active, grad_out, 0, 0)
    sum_inner = dot(grad_pre, normed_two, 0, 0)
    grad_hidden_part, sum_gain_two = norm_back(
        hidden, inverse_two, gain_two, dot(grad_pre, w_inner, 1, 1)
    )
    grad_hidden = grad_out.astype(F32) + grad_hidden_part
    grad_branch = grad_hidden.astype(BF)
    sum_output = dot(mix_flat, grad_branch, 1, 0)
    do_flat = dot(w_output, grad_branch, 1, 1).astype(BF)
    dq_flat, dk_rows, dv_rows, table_blocks = attend_back(
        q_flat, k_rows, v_rows, do_flat, mix_flat, stat, fq, fk, bias, row_len
    )
    sum_query = dot(normed, dq_flat, 0, 1)
    sum_key = dot(normed, dk_rows, 0, 0)
    sum_value = dot(normed, dv_rows, 0, 0)
    grad_normed = (
        dot(dq_flat, w_query, 0, 1) + dot(dk_rows, w_key, 1, 1) + dot(dv_rows, w_value, 1, 1)
    )
    grad_tokens_part, sum_gain_one = norm_back(wide, inverse_one, gain_one, grad_normed)
    grad_input = (grad_hidden + grad_tokens_part).astype(BF)
    sum_table = jnp.einsum(
        "zbfu,ibfu->zi", indicator.astype(F32), table_blocks, precision=lax.Precision.HIGHEST
    )

    scale = float(rows_dev * lax.axis_size("rows") * row_len) ** (-0.5)
    small = jnp.concatenate([sum_gain_one, sum_gain_two, sum_table.reshape(-1)])
    small = jnp.pad(small, (0, -small.size % (2 * CH * width))).reshape(-1, width)
    parts = (sum_outer, sum_inner, sum_output, sum_query, sum_key, sum_value, small)
    total = reduce_all(jnp.concatenate([g.astype(BF) for g in parts]), scale).astype(F32)
    out, at = [], 0
    for g in parts:
        out.append(total[at : at + g.shape[0]])
        at += g.shape[0]
    rest = out[6].reshape(-1)
    return (
        from_rows(result),
        from_rows(grad_input),
        out[3],
        out[4],
        out[5],
        out[2],
        out[1].T,
        out[0],
        rest[:width],
        rest[width : 2 * width],
        rest[2 * width : 2 * width + sum_table.size].reshape(sum_table.shape),
    )


def solution(mesh):
    tok = P("rows", "seq", None)
    in_specs = (tok, P("rows", None)) + (P(),) * 9 + (tok,)
    out_specs = (tok, tok) + (P(),) * 9
    return jax.shard_map(
        per_device, mesh=mesh, in_specs=in_specs, out_specs=out_specs, check_vma=False
    )
```

time: 1450 us -> 568 us (0.39)
  local copies, waits for them, and re-layouts: 589 us -> 87.7 us
  blocking collectives: 306 us -> 0 us
  Pallas kernels: 0 us -> 235 us
  matrix products: 328 us -> 144 us
  waiting for transfers between devices: 117 us -> 45.2 us
  other arithmetic: 71.8 us -> 23.5 us
  starting transfers between devices: 5.03 us -> 21.3 us
    unnamed x1 -> x0, blocking collectives: 306 us -> none
    pallas_call x0 -> x3, Pallas kernels: none -> 235 us  [the longest x1 168 us: reduce_ring(): pl.pallas_call(functools.partial(reduce_kernel, chunks, depth, scale), ou...]
    reshape x15 -> x3, local copies, waits for them, and re-layouts: 202 us -> 9.28 us  [the longest x2 9.16 us: from_rows(): array_in.reshape(mine, row_len, width)]
    dot_general x74 -> x20, matrix products: 328 us -> 144 us  [the longest x18 130 us: dot(): lax.dot_general(a, b, (((ca,), (cb,)), ((), ())), preferred_element_type=...]
    all_gather x7 -> x0, waiting for transfers between devices: 101 us -> none  [the longest x1 80.1 us: per_device(): lax.all_gather(grad_share.astype(jnp.bfloat16), ('rows', 'seq'), axis=0,...]
    unnamed x293 -> x84, local copies, waits for them, and re-layouts: 103 us -> 17.4 us
    transpose x1, local copies, waits for them, and re-layouts: 66.8 us -> 7.84 us  [per_device(): out[1]]
    slice x16 -> x6, local copies, waits for them, and re-layouts: 91.6 us -> 37.3 us  [the longest x2 20.5 us: per_device(): rest[2 * width:2 * width + sum_table.size].reshape(sum_table.shape)]
  transfers between devices with their start and end apart: 14 -> 4, of which waited for: 4 -> 2; matrix products, arithmetic and copies ran while one was open for 30% -> 29% of each run, Pallas kernels for 0% -> 36%
where the time goes in v2:
time: 568 us; the launch traced here: 558 us
  Pallas kernels  235 us (41%)
  matrix products  144 us (25%)
  local copies, waits for them, and re-layouts  87.7 us (15%)
  waiting for transfers between devices  45.2 us (8%)
  other arithmetic  23.5 us (4%)
  starting transfers between devices  21.3 us (4%)
    pallas_call x1, Pallas kernels, reduce_ring(): pl.pallas_call(functools.partial(reduce_kernel, chunks, depth, scale), ou...  168 us
    dot_general x18, matrix products, dot(): lax.dot_general(a, b, (((ca,), (cb,)), ((), ())), preferred_element_type=...  130 us
    all_to_all x2, waiting for transfers between devices, to_rows(): lax.all_to_all(array_in, 'seq', split_axis=0, concat_axis=1, tiled=True)  45.2 us
    pallas_call x1, Pallas kernels, attend(): pl.pallas_call(attend_kernel, grid=(pairs, row_count), in_specs=[flat, ro...  33.9 us
    pallas_call x1, Pallas kernels, attend_back(): pl.pallas_call(attend_back_kernel, grid=(pairs, row_count), in_specs=[fla...  33 us
    slice x2, local copies, waits for them, and re-layouts, per_device(): rest[2 * width:2 * width + sum_table.size].reshape(sum_table.shape)  20.5 us
    unnamed x84, local copies, waits for them, and re-layouts  17.4 us
    slice x3, local copies, waits for them, and re-layouts, per_device(): out.append(total[at:at + g.shape[0]])  15.4 us
  transfers between devices with their start and end apart: 4, of which 2 were waited for; matrix products, arithmetic and copies ran while one was open for 29% of the time, Pallas kernels for 36%

profile of v2, /device:TPU:1, one launch (start us, length us, event | category | flops | bytes accessed | tf_op | source)
XLA Modules:
  0.0 558.4 jit_solution(15758813177273319916)
XLA Ops:
  0.7 4.7 all-to-all-start
  6.1 27.2 %all-to-all-done = bf16[12,128,768]{2,1,0:T(8,128)(2,1)} async-done(((bf16[12,128,768]{2,1,0:T(8,128)(2,1)}), bf16[12,128,768]{2,1,0:T(8,128)(2,1)}, u32[]{:S(2)}, u32[]{:S(2)}) %all-to-all-start) | async-done | bytes 2359328 | tf_op jit(solution)/shard_map/all_to_all | solution.py:472
  33.3 5.7 %all-to-all-start.2 = ((bf16[12,128,768]{2,1,0:T(8,128)(2,1)}), bf16[12,128,768]{2,1,0:T(8,128)(2,1)}, u32[]{:S(2)}, u32[]{:S(2)}) async-start(bf16[12,128,768]{2,1,0:T(8,128)(2,1)} %param.23), calls=%async_computation.2 | async-start | bytes 4718592 | tf_op jit(solution)/shard_map/all_to_all | solution.py:472
  39.9 2.2 fusion.16
  42.2 4.4 fusion.20.bias_ref
  46.6 2.2 multiply_reduce_fusion.3
  48.8 18.0 %all-to-all-done.2 = bf16[12,128,768]{2,1,0:T(8,128)(2,1)} async-done(((bf16[12,128,768]{2,1,0:T(8,128)(2,1)}), bf16[12,128,768]{2,1,0:T(8,128)(2,1)}, u32[]{:S(2)}, u32[]{:S(2)}) %all-to-all-start.2) | async-done | bytes 2359328 | tf_op jit(solution)/shard_map/all_to_all | solution.py:472
  66.8 1.8 copy.69
  68.6 3.0 copy.62
  72.2 3.4 convolution_convert_fusion.3.v_ref
  75.6 3.4 convolution_convert_fusion.4.k_ref
  79.0 2.2 fusion.32.q_ref
  81.2 33.9 %shard_map.203 = (bf16[768,1536]{1,0:T(8,128)(2,1)S(1)}, f32[3,6,2,512]{3,2,1,0:T(2,128)S(1)}) custom-call(bf16[768,1536]{1,0:T(8,128)(2,1)S(1)} %fusion.32.q_ref, bf16[1536,768]{1,0:T(8,128)(2,1)} %convolution_convert_fusion.4.k_ref, bf16[1536,768]{1,0:T(8,128)(2,1)} %convolution_convert_fusion.3.v_ref, bf16[3,64,512]{2,1,0:T(8,128)(2,1)S(1)} %fusion.61.fq_ref, ...), custom_call_target="tpu_custom_call" | custom-call | flops 9663676416 | bytes 9437184 | tf_op jit(solution)/shard_map/pallas_call | solution.py:210
  115.2 2.2 multiply_reduce_fusion.2
  117.4 2.1 copy-done.14
  119.5 13.3 %fusion.63 = f32[1536,3072]{1,0:T(8,128)} fusion(bf16[768,3072]{1,0:T(8,128)(2,1)} %param.18, f32[1536,768]{1,0:T(8,128)S(1)} %get-tuple-element.80, f32[768]{0:T(1024)S(1)} %convert_element_type.185, f32[1536]{0:T(1024)S(1)} %get-tuple-element.78), kind=kOutput, calls=%fused_computation.113 | convolution fusion | flops 7251296256 | bytes 28320768 | tf_op jit(solution)/shard_map/dot_general | solution.py:64
  132.9 15.5 %add_convert_fusion = bf16[1536,768]{1,0:T(8,128)(2,1)S(1)} fusion(f32[1536,768]{1,0:T(8,128)} %copy-done.14, bf16[3072,768]{1,0:T(8,128)(2,1)S(1)} %bitcast.109, f32[1536,3072]{1,0:T(8,128)} %fusion.63), kind=kOutput, calls=%fused_computation.49 | convolution fusion | flops 7292583936 | bytes 30670848 | tf_op jit(solution)/shard_map/dot_general | solution.py:64
  148.3 20.3 %fusion.14 = bf16[1536,3072]{1,0:T(8,128)(2,1)} fusion(f32[1536,3072]{1,0:T(8,128)} %fusion.63, bf16[1536,768]{1,0:T(8,128)(2,1)S(1)} %bitcast.99, bf16[3072,768]{1,0:T(8,128)(2,1)S(1)} %bitcast.109), kind=kOutput, calls=%fused_computation.17 | convolution fusion | flops 7337410560 | bytes 35389440 | tf_op jit(solution)/shard_map/dot_general | solution.py:64
  168.6 15.4 %fusion.22 = bf16[9728,768]{1,0:T(8,128)(2,1)} fusion(bf16[1536,768]{1,0:T(8,128)(2,1)S(1)} %bitcast.100, f32[1536,3072]{1,0:T(8,128)} %fusion.63), kind=kOutput, calls=%fused_computation.30 | convolution fusion | flops 7292583936 | bytes 25952256 | tf_op jit(solution)/shard_map/dot_general | solution.py:64
  184.0 3.7 copy.67
  187.7 5.9 %all-to-all-start.1 = ((bf16[3,512,768]{2,0,1:T(4,128)(2,1)}), bf16[3,512,768]{2,0,1:T(4,128)(2,1)}, u32[]{:S(2)}, u32[]{:S(2)}) async-start(bf16[3,512,768]{2,0,1:T(4,128)(2,1)} %copy.67), calls=%async_computation.1 | async-start | bytes 6291456 | tf_op jit(solution)/shard_map/all_to_all | solution.py:476
  193.6 12.7 %multiply_reduce_fusion = (bf16[768]{0:T(1024)(128)(2,1)S(1)}, f32[1536]{0:T(1024)S(1)}, f32[1536,768]{1,0:T(8,128)S(1)}) fusion(f32[1536,768]{1,0:T(8,128)} %copy-done.14, f32[1536]{0:T(1024)S(1)} %get-tuple-element.78, f32[768]{0:T(1024)S(1)} %convert_element_type.185, bf16[1536,3072]{1,0:T(8,128)(2,1)} %fusion.14, bf16[768,3072]{1,0:T(8,128)(2,1)} %param.18), kind=kOutput, calls=%fused_computation.45 | convolution fusion | flops 7254832640 | bytes 23609856 | tf_op jit(solution)/shard_map/dot_general | solution.py:64
  206.4 13.5 %fusion.21 = bf16[9728,768]{1,0:T(8,128)(2,1)} fusion(bf16[9728,768]{1,0:T(8,128)(2,1)} %fusion.22, bf16[1536,3072]{1,0:T(8,128)(2,1)} %fusion.14, f32[1536,768]{1,0:T(8,128)} %copy-done.14, f32[768]{0:T(1024)S(1)} %convert_element_type.185, f32[1536]{0:T(1024)S(1)} %get-tuple-element.78), kind=kOutput, calls=%fused_computation.28 | convolution fusion | flops 7253655552 | bytes 18883584 | tf_op jit(solution)/shard_map/dot_general | solution.py:64
  220.0 1.5 subtract_add_fusion
  221.5 3.5 fusion.33.do_ref
  225.0 33.0 %shard_map.204 = (bf16[768,1536]{1,0:T(8,128)(2,1)S(1)}, bf16[1536,768]{1,0:T(8,128)(2,1)S(1)}, bf16[1536,768]{1,0:T(8,128)(2,1)}, f32[12,7,128,128]{3,2,1,0:T(8,128)}) custom-call(bf16[768,1536]{1,0:T(8,128)(2,1)} %copy-done.8, bf16[1536,768]{1,0:T(8,128)(2,1)} %convolution_convert_fusion.4.k_ref, bf16[1536,768]{1,0:T(8,128)(2,1)} %convolution_convert_fusion.3.v_ref, ...), custom_call_target="tpu_custom_call" | custom-call | flops 24159191040 | bytes 18874368 | tf_op jit(solution)/shard_map/pallas_call | solution.py:232
  260.8 11.6 %fusion.46 = bf16[32,12]{0,1:T(8,128)(2,1)S(1)} fusion(f32[12,7,128,128]{3,2,1,0:T(8,128)} %get-tuple-element.22, s32[7,128,128]{2,1,0:T(8,128)S(1)} %copy-done.16), kind=kOutput, calls=%fused_computation.75 | convolution fusion | flops 532152704 | bytes 5964544 | tf_op jit(solution)/shard_map/zbfu,ibfu->zi/dot_general | solution.py:541
  272.7 3.5 fusion.68
  276.2 2.1 fusion.67
  278.4 6.5 %fusion.31 = (bf16[768]{0:T(1024)(128)(2,1)S(1)}, f32[1536]{0:T(1024)S(1)}, f32[1536,768]{1,0:T(8,128)S(1)}) fusion(f32[4,3,128,768]{3,2,0,1:T(8,128)} %copy-done.10, f32[1536]{0:T(1024)S(1)} %copy-done.22, f32[768]{0:T(1024)S(1)} %copy-done.24, bf16[1536,768]{1,0:T(8,128)(2,1)} %get-tuple-element.21, bf16[768,768]{1,0:T(8,128)(2,1)S(1)} %copy-done, ...), kind=kOutput, calls=%fused_computation.44 | convolution fusion | flops 1821374208 | bytes 22430208 | tf_op jit(solution)/shard_map/dot_general | solution.py:64
  285.0 2.6 fusion.28
  288.5 3.1 fusion.40
  291.5 2.5 convert_element_type.201
  294.0 5.5 copy.71
  299.5 3.1 fusion.39
  302.5 3.1 fusion.38
  305.6 3.1 fusion.37
  308.8 5.0 all-to-all-start.3
  314.8 168.2 %shard_map.205 = bf16[9728,768]{1,0:T(8,128)(2,1)} custom-call(bf16[9728,768]{1,0:T(8,128)(2,1)} %constant_dynamic-update-slice_fusion.in_ref), custom_call_target="tpu_custom_call" | custom-call | tf_op jit(solution)/shard_map/pallas_call | solution.py:423
  484.3 8.0 %slice.59 = f32[3072,768]{1,0:T(8,128)} slice(bf16[9728,768]{1,0:T(8,128)(2,1)} %shard_map.205), slice={[0:3072], [0:768]} | slice | bytes 18874368 | tf_op jit(solution)/shard_map/slice | solution.py:552
  492.3 2.1 copy-done.9
  494.3 10.1 %convert_element_type.202 = f32[9728,768]{1,0:T(8,128)} convert(bf16[9728,768]{1,0:T(8,128)(2,1)S(1)} %copy-done.9) | non-fusion elementwise | flops 7471104 | bytes 44826624 | tf_op jit(solution)/shard_map/convert_element_type | solution.py:549
  504.4 7.8 %slice_bitcast_fusion = f32[768,3072]{0,1:T(8,128)} fusion(f32[9728,768]{1,0:T(8,128)} %convert_element_type.202), kind=kLoop, calls=%fused_computation.21 | loop fusion | bytes 18874368 | tf_op jit(solution)/shard_map/transpose | solution.py:562
  512.2 9.6 %copy.75 = f32[768,3072]{1,0:T(8,128)} copy(f32[768,3072]{0,1:T(8,128)} %slice_bitcast_fusion) | data formatting | bytes 18874368
  521.8 19.8 %slice.52 = f32[32768,12]{1,0:T(8,128)} reshape(f32[512,768]{1,0:T(8,128)S(1)} %slice.62) | data formatting | bytes 3145728 | tf_op jit(solution)/shard_map/slice | solution.py:566
  544.4 6.2 %fusion.66 = (f32[768,768]{1,0:T(8,128)}, f32[768,768]{1,0:T(8,128)}, f32[768,768]{1,0:T(8,128)}, f32[768,768]{1,0:T(8,128)}) fusion(bf16[9728,768]{1,0:T(8,128)(2,1)} %shard_map.205), kind=kLoop, calls=%fused_computation.114 | loop fusion | bytes 18874368 | tf_op jit(solution)/shard_map/slice | solution.py:552
  550.6 3.7 copy.68
  554.3 3.7 copy.72
  (117 shorter events, 11.2 us)
Async XLA Ops:
  0.6 71.5 %copy-start = (bf16[768,768]{1,0:T(8,128)(2,1)S(1)}, bf16[768,768]{1,0:T(8,128)(2,1)}, u32[]{:S(2)}) copy-start(bf16[768,768]{1,0:T(8,128)(2,1)} %param.16) | copy-start | bytes 3538948
  0.7 4.7 copy-start.26
  0.7 38.5 %copy-start.27 = (bf16[768]{0:T(1024)(128)(2,1)S(1)}, bf16[768]{0:T(1024)(128)(2,1)}, u32[]{:S(2)}) copy-start(bf16[768]{0:T(1024)(128)(2,1)} %param.21) | copy-start | bytes 4612
  0.7 38.5 %copy-start.28 = (bf16[768]{0:T(1024)(128)(2,1)S(1)}, bf16[768]{0:T(1024)(128)(2,1)}, u32[]{:S(2)}) copy-start(bf16[768]{0:T(1024)(128)(2,1)} %param.20) | copy-start | bytes 4612
  0.7 39.2 %copy-start.25 = (bf16[32,12]{0,1:T(8,128)(2,1)S(1)}, bf16[32,12]{0,1:T(8,128)(2,1)}, u32[]{:S(2)}) copy-start(bf16[32,12]{0,1:T(8,128)(2,1)} %param.22) | copy-start | bytes 2308
  0.7 32.6 %all-to-all-start = ((bf16[12,128,768]{2,1,0:T(8,128)(2,1)}), bf16[12,128,768]{2,1,0:T(8,128)(2,1)}, u32[]{:S(2)}, u32[]{:S(2)}) async-start(bf16[12,128,768]{2,1,0:T(8,128)(2,1)} %param.12), calls=%async_computation | async-start | bytes 4718592 | tf_op jit(solution)/shard_map/all_to_all | solution.py:472
  33.3 33.5 %all-to-all-start.2 = ((bf16[12,128,768]{2,1,0:T(8,128)(2,1)}), bf16[12,128,768]{2,1,0:T(8,128)(2,1)}, u32[]{:S(2)}, u32[]{:S(2)}) async-start(bf16[12,128,768]{2,1,0:T(8,128)(2,1)} %param.23), calls=%async_computation.2 | async-start | bytes 4718592 | tf_op jit(solution)/shard_map/all_to_all | solution.py:472
  39.1 32.5 %copy-start.23 = (f32[768]{0:T(1024)}, f32[768]{0:T(1024)S(1)}, u32[]{:S(2)}) copy-start(f32[768]{0:T(1024)S(1)} %convert_element_type.169) | copy-start | bytes 9220
  39.9 6.7 %copy-start.15 = (s32[7,128,128]{2,1,0:T(8,128)}, s32[7,128,128]{2,1,0:T(8,128)S(1)}, u32[]{:S(2)}) copy-start(s32[7,128,128]{2,1,0:T(8,128)S(1)} %fusion.51) | copy-start | bytes 1376260
  48.8 22.8 %copy-start.21 = (f32[1536]{0:T(1024)}, f32[1536]{0:T(1024)S(1)}, u32[]{:S(2)}) copy-start(f32[1536]{0:T(1024)S(1)} %rsqrt.26) | copy-start | bytes 18436
  68.6 100.0 %copy-start.12 = (bf16[4,3,128,768]{3,2,0,1:T(8,128)(2,1)}, bf16[4,3,128,768]{3,2,0,1:T(8,128)(2,1)S(1)}, u32[]{:S(2)}) copy-start(bf16[4,3,128,768]{3,2,0,1:T(8,128)(2,1)S(1)} %copy.69) | copy-start | bytes 7077892
  71.6 43.5 %copy-start.10 = (f32[4,3,128,768]{3,2,0,1:T(8,128)}, f32[4,3,128,768]{3,2,0,1:T(8,128)S(1)}, u32[]{:S(2)}) copy-start(f32[4,3,128,768]{3,2,0,1:T(8,128)S(1)} %copy.62) | copy-start | bytes 14155780
  72.1 6.9 %copy-start.18 = (bf16[1536,768]{1,0:T(8,128)(2,1)}, bf16[1536,768]{1,0:T(8,128)(2,1)S(1)}, u32[]{:S(2)}) copy-start(bf16[1536,768]{1,0:T(8,128)(2,1)S(1)} %fusion.24) | copy-start | bytes 7077892
  72.1 3.4 copy-start.30
  75.6 3.4 copy-start.31
  81.2 33.9 %copy-start.8 = (bf16[768,1536]{1,0:T(8,128)(2,1)}, bf16[768,1536]{1,0:T(8,128)(2,1)S(1)}, u32[]{:S(2)}) copy-start(bf16[768,1536]{1,0:T(8,128)(2,1)S(1)} %fusion.32.q_ref) | copy-start | bytes 7077892
  81.2 33.9 %copy-start.29 = (bf16[768,768]{1,0:T(8,128)(2,1)S(1)}, bf16[768,768]{1,0:T(8,128)(2,1)}, u32[]{:S(2)}) copy-start(bf16[768,768]{1,0:T(8,128)(2,1)} %param.17) | copy-start | bytes 3538948
  115.1 2.3 copy-start.3
  115.2 17.7 %slice-start.6 = ((s8[4718592]{0:T(1024)(128)(4,1)}), s8[524288]{0:T(1024)(128)(4,1)S(1)}, s32[]{:S(2)}) async-start(s8[4718592]{0:T(1024)(128)(4,1)} %bitcast.108), calls=%async_computation.10 | async-start | bytes 1048576
  117.4 2.1 copy-start.14
  119.5 13.3 %slice-start.7 = ((s8[4718592]{0:T(1024)(128)(4,1)}), s8[4194304]{0:T(1024)(128)(4,1)S(1)}, s32[]{:S(2)}) async-start(s8[4718592]{0:T(1024)(128)(4,1)} %bitcast.108), calls=%async_computation.11 | async-start | bytes 8388608
  187.7 121.1 %all-to-all-start.1 = ((bf16[3,512,768]{2,0,1:T(4,128)(2,1)}), bf16[3,512,768]{2,0,1:T(4,128)(2,1)}, u32[]{:S(2)}, u32[]{:S(2)}) async-start(bf16[3,512,768]{2,0,1:T(4,128)(2,1)} %copy.67), calls=%async_computation.1 | async-start | bytes 6291456 | tf_op jit(solution)/shard_map/all_to_all | solution.py:476
  193.6 26.3 %slice-start.4 = ((s8[4718592]{0:T(1024)(128)(4,1)}), s8[524288]{0:T(1024)(128)(4,1)S(1)}, s32[]{:S(2)}) async-start(s8[4718592]{0:T(1024)(128)(4,1)} %bitcast.102), calls=%async_computation.8 | async-start | bytes 1048576
  206.4 13.6 %copy-start.13 = (bf16[4,3,128,768]{3,2,0,1:T(8,128)(2,1)S(1)}, bf16[4,3,128,768]{3,2,0,1:T(8,128)(2,1)}, u32[]{:S(2)}) copy-start(bf16[4,3,128,768]{3,2,0,1:T(8,128)(2,1)} %copy-done.12) | copy-start | bytes 7077892
  206.4 13.6 %slice-start.5 = ((s8[4718592]{0:T(1024)(128)(4,1)}), s8[4194304]{0:T(1024)(128)(4,1)S(1)}, s32[]{:S(2)}) async-start(s8[4718592]{0:T(1024)(128)(4,1)} %bitcast.102), calls=%async_computation.9 | async-start | bytes 8388608
  221.5 3.5 copy-start.11
  225.0 35.8 %copy-start.16 = (s32[7,128,128]{2,1,0:T(8,128)S(1)}, s32[7,128,128]{2,1,0:T(8,128)}, u32[]{:S(2)}) copy-start(s32[7,128,128]{2,1,0:T(8,128)} %copy-done.15) | copy-start | bytes 1376260
  257.9 1.4 copy-start.1
  259.4 1.4 copy-start.5
  260.8 11.9 %copy-start.2 = (bf16[1536,768]{1,0:T(8,128)(2,1)S(1)}, bf16[1536,768]{1,0:T(8,128)(2,1)}, u32[]{:S(2)}) copy-start(bf16[1536,768]{1,0:T(8,128)(2,1)} %copy-done.1) | copy-start | bytes 7077892
  272.6 3.5 copy-start.6
  272.7 3.5 copy-start.32
  276.2 2.2 copy-start.22
  276.2 2.1 copy-start.24
  276.2 8.7 %slice-start = ((s8[4718592]{0:T(1024)(128)(4,1)}), s8[4194304]{0:T(1024)(128)(4,1)S(1)}, s32[]{:S(2)}) async-start(s8[4718592]{0:T(1024)(128)(4,1)} %bitcast.95), calls=%async_computation.4 | async-start | bytes 8388608
  276.2 8.7 %slice-start.2 = ((s8[4718592]{0:T(1024)(128)(4,1)}), s8[4194304]{0:T(1024)(128)(4,1)S(1)}, s32[]{:S(2)}) async-start(s8[4718592]{0:T(1024)(128)(4,1)} %bitcast.97), calls=%async_computation.6 | async-start | bytes 8388608
  278.4 6.6 %slice-start.1 = ((s8[4718592]{0:T(1024)(128)(4,1)}), s8[524288]{0:T(1024)(128)(4,1)S(1)}, s32[]{:S(2)}) async-start(s8[4718592]{0:T(1024)(128)(4,1)} %bitcast.95), calls=%async_computation.5 | async-start | bytes 1048576
  278.4 6.6 %slice-start.3 = ((s8[4718592]{0:T(1024)(128)(4,1)}), s8[524288]{0:T(1024)(128)(4,1)S(1)}, s32[]{:S(2)}) async-start(s8[4718592]{0:T(1024)(128)(4,1)} %bitcast.97), calls=%async_computation.7 | async-start | bytes 1048576
  284.9 3.5 copy-start.4
  294.0 5.5 copy-start.7
  294.0 5.5 copy-start.19
  302.5 3.1 copy-start.20
  308.8 5.1 copy-start.17
  308.8 245.5 %all-to-all-start.3 = ((bf16[3,512,768]{2,0,1:T(4,128)(2,1)}), bf16[3,512,768]{2,0,1:T(4,128)(2,1)}, u32[]{:S(2)}, u32[]{:S(2)}) async-start(bf16[3,512,768]{2,0,1:T(4,128)(2,1)} %copy.71), calls=%async_computation.3 | async-start | bytes 6291456 | tf_op jit(solution)/shard_map/all_to_all | solution.py:476
  484.3 10.1 %copy-start.9 = (bf16[9728,768]{1,0:T(8,128)(2,1)S(1)}, bf16[9728,768]{1,0:T(8,128)(2,1)}, u32[]{:S(2)}) copy-start(bf16[9728,768]{1,0:T(8,128)(2,1)} %shard_map.205) | copy-start | bytes 44826628
